TPU v7x, 128 devices: a whole 4x4x4 slice. The times are simulated.
128 devices in a mesh: pts: 32 (over z, y, core), grp: 4 (over x).
Axes of the slice: x: 4, y: 4, z: 4, core: 2. Of those that a mesh axis runs over, the one named last changes fastest.
Arguments:
- nodes: bfloat16 [2, 131072, 256], P(None, ('pts', 'grp')), may hold values from -6 to 6
- cotangent: bfloat16 [2, 131072, 256], P(None, ('pts', 'grp')), may hold values from -6 to 6
- first_inward: bfloat16 [256, 768], replicated, may hold values from -0.375 to 0.375
- first_outward: bfloat16 [256, 256], replicated, may hold values from -0.375 to 0.375
- second_inward: bfloat16 [256, 768], replicated, may hold values from -0.375 to 0.375
- second_outward: bfloat16 [256, 256], replicated, may hold values from -0.375 to 0.375
- rotated_source: int32 [2, 131072], P(None, ('pts', 'grp')), may hold values from 0 to 131071, as said below
- rotated_index: int32 [2, 131072], P(None, ('pts', 'grp')), may hold values from 0 to 131071, as said below
Outputs:
- input_grad: bfloat16 [2, 131072, 256], P(None, ('pts', 'grp'))
- first_inward_grad: float32 [256, 768], replicated
- first_outward_grad: float32 [256, 256], replicated
- second_inward_grad: float32 [256, 768], replicated
- second_outward_grad: float32 [256, 256], replicated
Inputs may be any that keep to these rules, and one draw needn't show every extreme that they name: For each sample, rotated_source and rotated_index are inverse permutations of the 131072 node indices. Split the indices into 128 aligned runs of 1024, one a device in the order of pts+grp. A node of run s has its rotated position in run t only where t - s, taken modulo 128, lies within -8 to 8. For every pair of different runs, at most 32 nodes of the first have their rotated position in the second, and exactly 32 for some pair. `rotated_index`: the inverse of rotated_source, sample by sample.
All inputs are finite; a program needn't handle non-finite values.
Results may differ from a plain program's by a relative error of at most 0.014.
Values may be sent and summed in bfloat16 or wider, within the bound.
No kernel may reach another device: no remote copies, remote signals or barrier semaphores. Data moves between devices by JAX's collectives and lax.ppermute only.
A program may use at most 128 MiB of HBM per device.

v0:
```python
import math

import jax
import jax.numpy as jnp
from jax import lax
from jax.sharding import PartitionSpec as P

HEADS = 8
BALL = 256
SPAN = 8
CAP = 32


EPSILON = 1e-06


def shifted(value, axis, steps):
    count = lax.axis_size(axis)
    pairs = [(source, (source + steps) % count) for source in range(count)]
    return lax.ppermute(value, axis, pairs)


def batched(pattern, left_side, right_side):
    return jnp.einsum(pattern, left_side, right_side, preferred_element_type=jnp.float32)


def rows_product(left_side, right_side):
    return lax.dot_general(
        left_side, right_side, (((0,), (0,)), ((), ())), preferred_element_type=jnp.float32
    )


def back_product(left_side, right_side):
    return lax.dot_general(
        left_side, right_side, (((1,), (1,)), ((), ())), preferred_element_type=jnp.float32
    )


def split_heads(matrix):
    return matrix.reshape(matrix.shape[0] // (2 * BALL), 2, BALL, HEADS, matrix.shape[1] // HEADS)


def join_heads(grouped):
    return grouped.reshape(-1, grouped.shape[3] * grouped.shape[4])


def attend_forward(pieces):
    queries, key_rows, values = pieces
    scores = batched("bqhd,bkhd->bhqk", queries, key_rows)
    weights = jnp.exp(scores)
    totals = jnp.sum(weights, axis=-1, keepdims=True)
    prob_low = (weights / totals).astype(jnp.bfloat16)
    result = batched("bhqk,bkhd->bqhd", prob_low, values)
    return (result.astype(jnp.bfloat16), totals)


def attend_backward(pieces):
    queries, key_rows, values, totals, grad_out = pieces
    scores = batched("bqhd,bkhd->bhqk", queries, key_rows)
    prob_full = jnp.exp(scores) / totals
    prob_low = prob_full.astype(jnp.bfloat16)
    grad_values = batched("bhqk,bqhd->bkhd", prob_low, grad_out)
    grad_probs = batched("bqhd,bkhd->bhqk", grad_out, values)
    column_sum = jnp.sum(grad_probs * prob_full, axis=-1, keepdims=True)
    grad_scores = (prob_full * (grad_probs - column_sum)).astype(jnp.bfloat16)
    grad_queries = batched("bhqk,bkhd->bqhd", grad_scores, key_rows)
    grad_keys = batched("bhqk,bqhd->bkhd", grad_scores, queries)
    return (grad_queries, grad_keys, grad_values)


def block_forward(row_block, inward):
    feature_width = row_block.shape[1]
    widened = row_block.astype(jnp.float32)
    row_scale = lax.rsqrt(jnp.mean(widened * widened, axis=-1, keepdims=True) + EPSILON)
    normed = (widened * row_scale).astype(jnp.bfloat16)
    mixture = jnp.dot(normed, inward, preferred_element_type=jnp.float32)
    query_raw = mixture[:, :feature_width]
    key_raw = mixture[:, feature_width : 2 * feature_width]
    value_raw = mixture[:, 2 * feature_width :]
    query_scale = lax.rsqrt(jnp.mean(query_raw * query_raw, axis=-1, keepdims=True) + EPSILON)
    query_unit = query_raw * query_scale
    key_scale = lax.rsqrt(jnp.mean(key_raw * key_raw, axis=-1, keepdims=True) + EPSILON)
    key_unit = key_raw * key_scale
    head_factor = (feature_width // HEADS) ** (-0.5)
    queries = (query_unit * head_factor).astype(jnp.bfloat16)
    key_rows = key_unit.astype(jnp.bfloat16)
    values = value_raw.astype(jnp.bfloat16)
    attended, totals = lax.map(
        attend_forward, (split_heads(queries), split_heads(key_rows), split_heads(values))
    )
    attended = join_heads(attended)
    return (
        widened,
        row_scale,
        normed,
        query_unit,
        query_scale,
        key_unit,
        key_scale,
        queries,
        key_rows,
        values,
        totals,
        attended,
    )


def block_output(stashed, outward):
    widened = stashed[0]
    attended = stashed[11]
    return (widened + jnp.dot(attended, outward, preferred_element_type=jnp.float32)).astype(
        jnp.bfloat16
    )


def block_backward(stashed, inward, outward, grad_rows):
    (
        widened,
        row_scale,
        normed,
        query_unit,
        query_scale,
        key_unit,
        key_scale,
        queries,
        key_rows,
        values,
        totals,
        attended,
    ) = stashed
    feature_width = widened.shape[1]
    grad_outward = rows_product(attended, grad_rows)
    grad_attended = back_product(grad_rows, outward).astype(jnp.bfloat16)
    grad_queries, grad_keys, grad_values = lax.map(
        attend_backward,
        (
            split_heads(queries),
            split_heads(key_rows),
            split_heads(values),
            totals,
            split_heads(grad_attended),
        ),
    )
    grad_queries = join_heads(grad_queries) * (feature_width // HEADS) ** (-0.5)
    grad_keys = join_heads(grad_keys)
    grad_values = join_heads(grad_values)
    grad_qraw = query_scale * (
        grad_queries - query_unit * jnp.mean(grad_queries * query_unit, axis=-1, keepdims=True)
    )
    grad_kraw = key_scale * (
        grad_keys - key_unit * jnp.mean(grad_keys * key_unit, axis=-1, keepdims=True)
    )
    grad_mixture = jnp.concatenate([grad_qraw, grad_kraw, grad_values], axis=1).astype(jnp.bfloat16)
    grad_inward = rows_product(normed, grad_mixture)
    grad_normed = back_product(grad_mixture, inward)
    unit_rows = widened * row_scale
    grad_input = grad_rows.astype(jnp.float32) + row_scale * (
        grad_normed - unit_rows * jnp.mean(grad_normed * unit_rows, axis=-1, keepdims=True)
    )
    return (grad_input.astype(jnp.bfloat16), grad_inward, grad_outward)


def pack_rows(row_array, slot_table, slot_total):

    def place_sample(sample_rows, sample_slots):
        empty = jnp.zeros((slot_total, sample_rows.shape[1]), sample_rows.dtype)
        return empty.at[sample_slots].set(sample_rows, mode="drop")

    return jax.vmap(place_sample)(row_array, slot_table)


def outbound(packets):
    classes = packets.shape[2]
    landed = []
    for place in range(classes):
        if place == SPAN:
            landed.append(jnp.zeros_like(packets[:, :, place]))
        else:
            landed.append(shifted(packets[:, :, classes - 1 - place], ("pts", "grp"), SPAN - place))
    return jnp.stack(landed, axis=2)


def inbound(packets):
    classes = packets.shape[1]
    landed = []
    for place in range(classes):
        if place == SPAN:
            landed.append(jnp.zeros_like(packets[:, place]))
        else:
            landed.append(shifted(packets[:, classes - 1 - place], ("pts", "grp"), SPAN - place))
    return jnp.stack(landed, axis=1)


def per_device(
    nodes,
    cotangent,
    first_inward,
    first_outward,
    second_inward,
    second_outward,
    rotated_source,
    rotated_index,
):
    samples_count, local_rows, feature_width = nodes.shape
    shard_count = lax.axis_size(("pts", "grp"))
    own_index = lax.axis_index(("pts", "grp"))
    classes = 2 * SPAN + 1
    slot_total = classes * CAP
    first_stash = block_forward(nodes.reshape(-1, feature_width), first_inward)
    after_first = block_output(first_stash, first_outward).reshape(
        samples_count, local_rows, feature_width
    )
    target_class = (rotated_index // local_rows - own_index + SPAN) % shard_count
    class_ids = jnp.arange(classes, dtype=jnp.int32)
    target_hits = (target_class[:, :, None] == class_ids[None, None, :]).astype(jnp.int32)
    send_rank = jnp.sum(jnp.cumsum(target_hits, axis=1) * target_hits, axis=2) - 1
    stays_home = target_class == SPAN
    send_slot = jnp.where(stays_home, slot_total, target_class * CAP + send_rank)
    source_shard = rotated_source // local_rows
    source_class = (source_shard - own_index + SPAN) % shard_count
    same_source = source_shard[:, :, None] == source_shard[:, None, :]
    earlier = rotated_source[:, None, :] < rotated_source[:, :, None]
    receive_rank = jnp.sum((same_source & earlier).astype(jnp.int32), axis=2)
    from_home = source_class == SPAN
    receive_slot = jnp.where(from_home, slot_total, source_class * CAP + receive_rank)
    packets = jnp.stack(
        [
            pack_rows(after_first, send_slot, slot_total),
            pack_rows(cotangent, send_slot, slot_total),
        ],
        axis=0,
    )
    packets = packets.reshape(2, samples_count, classes, CAP, feature_width)
    arrived = outbound(packets).reshape(2, samples_count, slot_total, feature_width)
    pick_rotated = jnp.where(
        from_home, rotated_source - own_index * local_rows, local_rows + receive_slot
    )
    rotated = jnp.take_along_axis(
        jnp.concatenate([after_first, arrived[0]], axis=1), pick_rotated[:, :, None], axis=1
    )
    rotated_cot = jnp.take_along_axis(
        jnp.concatenate([cotangent, arrived[1]], axis=1), pick_rotated[:, :, None], axis=1
    )
    second_stash = block_forward(rotated.reshape(-1, feature_width), second_inward)
    rotated_grad, second_in_grad, second_out_grad = block_backward(
        second_stash, second_inward, second_outward, rotated_cot.reshape(-1, feature_width)
    )
    rotated_grad = rotated_grad.reshape(samples_count, local_rows, feature_width)
    back_packets = pack_rows(rotated_grad, receive_slot, slot_total).reshape(
        samples_count, classes, CAP, feature_width
    )
    returned = inbound(back_packets).reshape(samples_count, slot_total, feature_width)
    pick_after = jnp.where(
        stays_home, rotated_index - own_index * local_rows, local_rows + send_slot
    )
    grad_after = jnp.take_along_axis(
        jnp.concatenate([rotated_grad, returned], axis=1), pick_after[:, :, None], axis=1
    )
    input_grad, first_in_grad, first_out_grad = block_backward(
        first_stash, first_inward, first_outward, grad_after.reshape(-1, feature_width)
    )
    summed = lax.psum(
        (first_in_grad, first_out_grad, second_in_grad, second_out_grad), ("pts", "grp")
    )
    factor = 1.0 / math.sqrt(samples_count * local_rows * shard_count)
    return (
        input_grad.reshape(nodes.shape),
        summed[0] * factor,
        summed[1] * factor,
        summed[2] * factor,
        summed[3] * factor,
    )


def solution(mesh):
    in_specs = (
        P(None, ("pts", "grp"), None),
        P(None, ("pts", "grp"), None),
        P(),
        P(),
        P(),
        P(),
        P(None, ("pts", "grp")),
        P(None, ("pts", "grp")),
    )
    out_specs = (P(None, ("pts", "grp"), None), P(), P(), P(), P())
    return jax.shard_map(
        per_device, mesh=mesh, in_specs=in_specs, out_specs=out_specs, check_vma=False
    )
```

profile of v0, /device:TPU:1, one launch (start us, length us, event | category | flops | bytes accessed | tf_op | source)
XLA Modules:
  0.0 592.8 jit_solution(7289202582831580347)
XLA Ops:
  14.1 2.3 copy-done.1
  16.5 9.6 %reduce-window.6 = s32[2,17,8,128]{3,2,1,0:T(8,128)S(1)} reduce-window(s32[2,17,8,128]{3,2,1,0:T(8,128)S(1)} %fusion.88, s32[]{:T(128)} %copy.410), window={size=1x1x1x128 pad=0_0x0_0x0_0x127_0}, to_apply=%region_0.0 | reduce-window | flops 4421632 | bytes 278532 | tf_op jit(solution)/shard_map/reduce-window
  30.2 3.7 multiply_convert_fusion.7
  42.2 18.2 %while.52 = (s32[]{:T(128)}, bf16[4,2,256,8,32]{2,1,0,4,3:T(2,128)(2,1)S(1)}, f32[4,2,8,256,1]{3,2,1,4,0:T(8,128)}, bf16[4,2,256,8,32]{2,4,3,1,0:T(8,128)(2,1)},...) while((s32[]{:T(128)}, ...), condition=%wide.region_8.9_spmd, body=%wide.region_6.8_spmd.sunk | while | flops 137490432 | bytes 10029137 | solution.py:88
  61.7 2.4 fusion.72
  64.0 9.9 %scatter_custom_fusion = bf16[1088,256]{1,0:T(8,128)(2,1)S(1)} fusion(s32[2048]{0:T(1024)} %bitcast.558, bf16[2048,256]{1,0:T(8,128)(2,1)} %fusion.72, bf16[]{:T(256)} %constant.147.clone.1), kind=kCustom, calls=%fused_computation.153 | custom fusion | bytes 557568
  73.9 9.7 %scatter_custom_fusion.1 = bf16[1088,256]{1,0:T(8,128)(2,1)S(1)} fusion(s32[2048]{0:T(1024)} %bitcast.559, bf16[2048,256]{1,0:T(8,128)(2,1)} %bitcast.547, bf16[]{:T(256)} %constant.147.clone.1), kind=kCustom, calls=%fused_computation.151 | custom fusion | bytes 557568
  83.8 2.2 collective-permute-start
  86.0 4.3 collective-permute-start.1
  91.8 2.2 collective-permute-start.4
  103.8 4.7 collective-permute-start.10
  108.8 2.5 collective-permute-start.12
  111.4 2.1 collective-permute-start.13
  115.3 2.9 collective-permute-done.13
  122.1 11.1 %gather_fusion.1 = bf16[2048,256]{1,0:T(8,128)(2,1)S(1)} fusion(bf16[2,1568,256]{2,1,0:T(8,128)(2,1)S(1)} %pad_maximum_fusion.3, s32[2048]{0:T(1024)S(1)} %bitcast.525), kind=kCustom, calls=%fused_computation.1.clone | custom fusion | bytes 2113536 | tf_op jit(solution)/shard_map/jit(take_along_axis)/gather | solution.py:238
  141.5 2.6 reshape.225
  145.6 2.7 reshape.226
  148.2 2.4 copy.171
  152.8 16.7 %while.53 = (s32[]{:T(128)}, bf16[4,2,256,8,32]{2,1,0,4,3:T(2,128)(2,1)}, f32[4,2,8,256,1]{3,2,1,4,0:T(8,128)}, bf16[4,2,256,8,32]{2,4,3,1,0:T(8,128)(2,1)}, bf1...) while((s32[]{:T(128)}, ...), condition=%wide.region_17.19_spmd, body=%wide.region_15.18_spmd.sunk | while | flops 137490432 | bytes 10029645 | solution.py:88
  172.3 20.9 %gather_fusion = bf16[2048,256]{1,0:T(8,128)(2,1)} fusion(bf16[2,1568,256]{2,1,0:T(8,128)(2,1)S(1)} %pad_maximum_fusion.2, s32[2048]{0:T(1024)S(1)} %bitcast.526), kind=kCustom, calls=%fused_computation.clone | custom fusion | bytes 2113536 | tf_op jit(solution)/shard_map/jit(take_along_axis)/gather | solution.py:241
  202.1 40.6 %while.54 = (s32[]{:T(128)}, f32[4,2,256,8,32]{2,4,3,1,0:T(8,128)}, f32[4,2,256,8,32]{2,1,0,4,3:T(2,128)}, bf16[4,2,256,8,32]{2,4,3,1,0:T(8,128)(2,1)}, bf16[4,2...) while((s32[]{:T(128)}, f32[4,2,256,8,32]{2,4,3,1,0:T(8,128)}, ...), condition=%wide.region_20.22_spmd, body=%wide.region_18.21_spmd.sunk | while | flops 342880256 | bytes 36523632 | solution.py:134
  244.5 2.9 copy.179
  247.5 2.9 mul.262
  250.4 3.9 reshape.228
  254.3 3.6 multiply_reduce_fusion.7
  259.1 3.3 copy.181
  262.4 2.8 reshape.229
  265.2 4.1 multiply_convert_fusion.5
  274.3 10.3 %scatter_custom_fusion.2 = bf16[1088,256]{1,0:T(8,128)(2,1)} fusion(s32[2048]{0:T(1024)} %bitcast.557, bf16[2048,256]{1,0:T(8,128)(2,1)S(1)} %add_convert_fusion.1, bf16[]{:T(256)} %constant.147.clone.1), kind=kCustom, calls=%fused_computation.149 | custom fusion | bytes 557568
  288.7 3.6 collective-permute-start.18
  294.6 2.5 fusion.103
  302.7 3.0 collective-permute-start.24
  308.0 5.0 collective-permute-start.26
  313.4 3.7 collective-permute-start.28
  318.6 4.4 collective-permute-done.29
  324.0 20.8 %gather_fusion.2 = bf16[2048,256]{1,0:T(8,128)(2,1)} fusion(bf16[2,1568,256]{2,1,0:T(8,128)(2,1)S(1)} %pad_maximum_fusion.4, s32[2048]{0:T(1024)S(1)} %bitcast.527), kind=kCustom, calls=%fused_computation.2.clone | custom fusion | bytes 2113536 | tf_op jit(solution)/shard_map/jit(take_along_axis)/gather | solution.py:256
  350.5 2.0 broadcast.212.clone
  352.5 48.8 %while.55 = (s32[]{:T(128)}, f32[4,2,256,8,32]{2,4,3,1,0:T(8,128)S(1)}, f32[4,2,256,8,32]{2,1,0,4,3:T(2,128)}, bf16[4,2,256,8,32]{2,4,3,1,0:T(8,128)(2,1)}, bf16...) while((s32[]{:T(128)}, ...), condition=%wide.region_27.29_spmd, body=%wide.region_25.28_spmd.sunk | while | flops 342880256 | bytes 36524140 | solution.py:134
  401.7 3.0 copy.203
  404.7 2.9 mul.276
  407.7 4.2 reshape.235
  411.9 3.9 multiply_reduce_fusion.4
  417.0 2.0 copy.205
  419.0 2.6 reshape.236
  421.6 3.8 multiply_convert_fusion.3
  430.2 2.9 multiply_reduce_fusion.2
  434.8 146.1 %all-reduce.3.cloned.1.call-done = (f32[256,768]{1,0:T(8,128)}, f32[256,256]{1,0:T(8,128)}, f32[256,768]{1,0:T(8,128)}, f32[256,256]{1,0:T(8,128)}) async-done(((f32[256,768]{1,0:T(8,128)}, f32[256,256]{1,0:T(8,128)}, f32[256,768]{1,0:T(8,128)}, f32[256,256]{1,0:T(8,128)}), (f32[256,768]{1,0:T(8,128)}, f32[256,256]{1,0:T(8,128)}, f32[256,768]{1,0:T(8,128)}, ...) | async-done | bytes 2097168 | tf_op jit(solution)/shard_map/psum | solution.py:262
  580.9 2.2 broadcast_multiply_fusion.2
  (430 shorter events, 225.7 us)
Async XLA Ops:
  7.2 127.6 %copy-start = (bf16[256,768]{1,0:T(8,128)(2,1)S(1)}, bf16[256,768]{1,0:T(8,128)(2,1)}, u32[]{:S(2)}) copy-start(bf16[256,768]{1,0:T(8,128)(2,1)} %param.22) | copy-start | bytes 1179652
  7.2 573.7 %all-reduce.3.cloned.1.call-start = ((), (), s32[]{:S(2)}) async-start(), calls=%async_computation | async-start | bytes 4194304 | tf_op jit(solution)/shard_map/psum | solution.py:262
  16.3 12.5 %copy-start.67 = (s32[2]{0:T(128)S(1)}, s32[2]{0:T(128)}, u32[]{:S(2)}) copy-start(s32[2]{0:T(128)} %constant.171) | copy-start | bytes 28
  61.3 22.4 %copy-start.11 = (bf16[2048,256]{0,1:T(8,128)(2,1)}, bf16[2048,256]{0,1:T(8,128)(2,1)S(1)}, u32[]{:S(2)}) copy-start(bf16[2048,256]{0,1:T(8,128)(2,1)S(1)} %reshape.221) | copy-start | bytes 3145732
  64.0 30.1 %copy-start.51 = (s32[2,1024]{1,0:T(2,128)S(1)}, s32[2,1024]{1,0:T(2,128)}, u32[]{:S(2)}) copy-start(s32[2,1024]{1,0:T(2,128)} %copy-done.50) | copy-start | bytes 24580
  64.0 30.1 %copy-start.53 = (s32[2,1024]{1,0:T(2,128)S(1)}, s32[2,1024]{1,0:T(2,128)}, u32[]{:S(2)}) copy-start(s32[2,1024]{1,0:T(2,128)} %copy-done.52) | copy-start | bytes 24580
  83.8 12.8 %collective-permute-start = (bf16[2,2,32,256]{3,2,1,0:T(8,128)(2,1)S(1)}, bf16[2,2,32,256]{3,2,1,0:T(8,128)(2,1)S(1)}, u32[]{:S(2)}, u32[]{:S(2)}) collective-permute-start(bf16[2,2,32,256]{3,2,1,0:T(8,128)(2,1)S(1)} %get-tuple-element.385), channel_id=1, source_target_pairs={{0,8},{1,9},{2,10},{3,11},{4,12},{5,13},{6,14},{7,15},{8,16},{9,17... | collective-permute-start | bytes 196616 | tf_op jit(solution)/shard_map/ppermute | solution.py:20
  86.0 12.2 %collective-permute-start.1 = (bf16[2,2,32,256]{3,2,1,0:T(8,128)(2,1)S(1)}, bf16[2,2,32,256]{3,2,1,0:T(8,128)(2,1)S(1)}, u32[]{:S(2)}, u32[]{:S(2)}) collective-permute-start(bf16[2,2,32,256]{3,2,1,0:T(8,128)(2,1)S(1)} %get-tuple-element.384), channel_id=1, source_target_pairs={{0,7},{1,8},{2,9},{3,10},{4,11},{5,12},{6,13},{7,14},{8,15},{9,16}... | collective-permute-start | bytes 196616 | tf_op jit(solution)/shard_map/ppermute | solution.py:20
  90.3 9.4 %collective-permute-start.2 = (bf16[2,2,32,256]{3,2,1,0:T(8,128)(2,1)S(1)}, bf16[2,2,32,256]{3,2,1,0:T(8,128)(2,1)S(1)}, u32[]{:S(2)}, u32[]{:S(2)}) collective-permute-start(bf16[2,2,32,256]{3,2,1,0:T(8,128)(2,1)S(1)} %get-tuple-element.383), channel_id=1, source_target_pairs={{0,6},{1,7},{2,8},{3,9},{4,10},{5,11},{6,12},{7,13},{8,14},{9,15},... | collective-permute-start | bytes 196616 | tf_op jit(solution)/shard_map/ppermute | solution.py:20
  91.8 9.0 %collective-permute-start.3 = (bf16[2,2,32,256]{3,2,1,0:T(8,128)(2,1)S(1)}, bf16[2,2,32,256]{3,2,1,0:T(8,128)(2,1)S(1)}, u32[]{:S(2)}, u32[]{:S(2)}) collective-permute-start(bf16[2,2,32,256]{3,2,1,0:T(8,128)(2,1)S(1)} %get-tuple-element.382), channel_id=1, source_target_pairs={{0,5},{1,6},{2,7},{3,8},{4,9},{5,10},{6,11},{7,12},{8,13},{9,14},{... | collective-permute-start | bytes 196616 | tf_op jit(solution)/shard_map/ppermute | solution.py:20
  91.8 11.0 %collective-permute-start.4 = (bf16[2,2,32,256]{3,2,1,0:T(8,128)(2,1)S(1)}, bf16[2,2,32,256]{3,2,1,0:T(8,128)(2,1)S(1)}, u32[]{:S(2)}, u32[]{:S(2)}) collective-permute-start(bf16[2,2,32,256]{3,2,1,0:T(8,128)(2,1)S(1)} %get-tuple-element.381), channel_id=1, source_target_pairs={{0,4},{1,5},{2,6},{3,7},{4,8},{5,9},{6,10},{7,11},{8,12},{9,13},{1... | collective-permute-start | bytes 196616 | tf_op jit(solution)/shard_map/ppermute | solution.py:20
  94.9 39.2 %copy-start.34 = (pred[2,1024]{1,0:T(4,128)(4,1)}, pred[2,1024]{1,0:T(4,128)(4,1)S(1)}, u32[]{:S(2)}) copy-start(pred[2,1024]{1,0:T(4,128)(4,1)S(1)} %get-tuple-element.410) | copy-start | bytes 6148
  96.6 7.2 %collective-permute-start.5 = (bf16[2,2,32,256]{3,2,1,0:T(8,128)(2,1)S(1)}, bf16[2,2,32,256]{3,2,1,0:T(8,128)(2,1)S(1)}, u32[]{:S(2)}, u32[]{:S(2)}) collective-permute-start(bf16[2,2,32,256]{3,2,1,0:T(8,128)(2,1)S(1)} %get-tuple-element.380), channel_id=1, source_target_pairs={{0,3},{1,4},{2,5},{3,6},{4,7},{5,8},{6,9},{7,10},{8,11},{9,12},{10... | collective-permute-start | bytes 196616 | tf_op jit(solution)/shard_map/ppermute | solution.py:20
  98.2 10.3 %collective-permute-start.6 = (bf16[2,2,32,256]{3,2,1,0:T(8,128)(2,1)S(1)}, bf16[2,2,32,256]{3,2,1,0:T(8,128)(2,1)S(1)}, u32[]{:S(2)}, u32[]{:S(2)}) collective-permute-start(bf16[2,2,32,256]{3,2,1,0:T(8,128)(2,1)S(1)} %get-tuple-element.379), channel_id=1, source_target_pairs={{0,2},{1,3},{2,4},{3,5},{4,6},{5,7},{6,8},{7,9},{8,10},{9,11},{10,... | collective-permute-start | bytes 196616 | tf_op jit(solution)/shard_map/ppermute | solution.py:20
  99.7 9.1 %collective-permute-start.7 = (bf16[2,2,32,256]{3,2,1,0:T(8,128)(2,1)S(1)}, bf16[2,2,32,256]{3,2,1,0:T(8,128)(2,1)S(1)}, u32[]{:S(2)}, u32[]{:S(2)}) collective-permute-start(bf16[2,2,32,256]{3,2,1,0:T(8,128)(2,1)S(1)} %get-tuple-element.378), channel_id=1, source_target_pairs={{0,1},{1,2},{2,3},{3,4},{4,5},{5,6},{6,7},{7,8},{8,9},{9,10},{10,1... | collective-permute-start | bytes 196616 | tf_op jit(solution)/shard_map/ppermute | solution.py:20
  100.8 10.6 %collective-permute-start.8 = (bf16[2,2,32,256]{3,2,1,0:T(8,128)(2,1)S(1)}, bf16[2,2,32,256]{3,2,1,0:T(8,128)(2,1)S(1)}, u32[]{:S(2)}, u32[]{:S(2)}) collective-permute-start(bf16[2,2,32,256]{3,2,1,0:T(8,128)(2,1)S(1)} %get-tuple-element.377), channel_id=1, source_target_pairs={{0,127},{1,0},{2,1},{3,2},{4,3},{5,4},{6,5},{7,6},{8,7},{9,8},{10,... | collective-permute-start | bytes 196616 | tf_op jit(solution)/shard_map/ppermute | solution.py:20
  102.8 10.7 %collective-permute-start.9 = (bf16[2,2,32,256]{3,2,1,0:T(8,128)(2,1)S(1)}, bf16[2,2,32,256]{3,2,1,0:T(8,128)(2,1)S(1)}, u32[]{:S(2)}, u32[]{:S(2)}) collective-permute-start(bf16[2,2,32,256]{3,2,1,0:T(8,128)(2,1)S(1)} %get-tuple-element.376), channel_id=1, source_target_pairs={{0,126},{1,127},{2,0},{3,1},{4,2},{5,3},{6,4},{7,5},{8,6},{9,7},{1... | collective-permute-start | bytes 196616 | tf_op jit(solution)/shard_map/ppermute | solution.py:20
  103.8 10.7 %collective-permute-start.10 = (bf16[2,2,32,256]{3,2,1,0:T(8,128)(2,1)S(1)}, bf16[2,2,32,256]{3,2,1,0:T(8,128)(2,1)S(1)}, u32[]{:S(2)}, u32[]{:S(2)}) collective-permute-start(bf16[2,2,32,256]{3,2,1,0:T(8,128)(2,1)S(1)} %get-tuple-element.375), channel_id=1, source_target_pairs={{0,125},{1,126},{2,127},{3,0},{4,1},{5,2},{6,3},{7,4},{8,5},{9,6},... | collective-permute-start | bytes 196616 | tf_op jit(solution)/shard_map/ppermute | solution.py:20
  108.5 6.8 %collective-permute-start.11 = (bf16[2,2,32,256]{3,2,1,0:T(8,128)(2,1)S(1)}, bf16[2,2,32,256]{3,2,1,0:T(8,128)(2,1)S(1)}, u32[]{:S(2)}, u32[]{:S(2)}) collective-permute-start(bf16[2,2,32,256]{3,2,1,0:T(8,128)(2,1)S(1)} %get-tuple-element.374), channel_id=1, source_target_pairs={{0,124},{1,125},{2,126},{3,127},{4,0},{5,1},{6,2},{7,3},{8,4},{9,5... | collective-permute-start | bytes 196616 | tf_op jit(solution)/shard_map/ppermute | solution.py:20
  108.8 6.4 %collective-permute-start.12 = (bf16[2,2,32,256]{3,2,1,0:T(8,128)(2,1)S(1)}, bf16[2,2,32,256]{3,2,1,0:T(8,128)(2,1)S(1)}, u32[]{:S(2)}, u32[]{:S(2)}) collective-permute-start(bf16[2,2,32,256]{3,2,1,0:T(8,128)(2,1)S(1)} %get-tuple-element.373), channel_id=1, source_target_pairs={{0,123},{1,124},{2,125},{3,126},{4,127},{5,0},{6,1},{7,2},{8,3},{9... | collective-permute-start | bytes 196616 | tf_op jit(solution)/shard_map/ppermute | solution.py:20
  111.4 6.9 %collective-permute-start.13 = (bf16[2,2,32,256]{3,2,1,0:T(8,128)(2,1)S(1)}, bf16[2,2,32,256]{3,2,1,0:T(8,128)(2,1)S(1)}, u32[]{:S(2)}, u32[]{:S(2)}) collective-permute-start(bf16[2,2,32,256]{3,2,1,0:T(8,128)(2,1)S(1)} %get-tuple-element.372), channel_id=1, source_target_pairs={{0,122},{1,123},{2,124},{3,125},{4,126},{5,127},{6,0},{7,1},{8,2},... | collective-permute-start | bytes 196616 | tf_op jit(solution)/shard_map/ppermute | solution.py:20
  113.5 6.0 %collective-permute-start.14 = (bf16[2,2,32,256]{3,2,1,0:T(8,128)(2,1)S(1)}, bf16[2,2,32,256]{3,2,1,0:T(8,128)(2,1)S(1)}, u32[]{:S(2)}, u32[]{:S(2)}) collective-permute-start(bf16[2,2,32,256]{3,2,1,0:T(8,128)(2,1)S(1)} %get-tuple-element.371), channel_id=1, source_target_pairs={{0,121},{1,122},{2,123},{3,124},{4,125},{5,126},{6,127},{7,0},{8,1... | collective-permute-start | bytes 196616 | tf_op jit(solution)/shard_map/ppermute | solution.py:20
  114.5 6.6 %collective-permute-start.15 = (bf16[2,2,32,256]{3,2,1,0:T(8,128)(2,1)S(1)}, bf16[2,2,32,256]{3,2,1,0:T(8,128)(2,1)S(1)}, u32[]{:S(2)}, u32[]{:S(2)}) collective-permute-start(bf16[2,2,32,256]{3,2,1,0:T(8,128)(2,1)S(1)} %get-tuple-element.370), channel_id=1, source_target_pairs={{0,120},{1,121},{2,122},{3,123},{4,124},{5,125},{6,126},{7,127},{8... | collective-permute-start | bytes 196616 | tf_op jit(solution)/shard_map/ppermute | solution.py:20
  172.3 20.9 %copy-start.35 = (pred[2,1024]{1,0:T(4,128)(4,1)S(1)}, pred[2,1024]{1,0:T(4,128)(4,1)}, u32[]{:S(2)}) copy-start(pred[2,1024]{1,0:T(4,128)(4,1)} %copy-done.34) | copy-start | bytes 6148
  274.3 18.7 %copy-start.22 = (bf16[4,2,256,8,32]{2,1,0,4,3:T(2,128)(2,1)S(1)}, bf16[4,2,256,8,32]{2,1,0,4,3:T(2,128)(2,1)}, u32[]{:S(2)}) copy-start(bf16[4,2,256,8,32]{2,1,0,4,3:T(2,128)(2,1)} %get-tuple-element.179) | copy-start | bytes 3145732
  286.4 10.7 %collective-permute-start.16 = (bf16[2,32,256]{2,1,0:T(8,128)(2,1)}, bf16[2,32,256]{2,1,0:T(8,128)(2,1)}, u32[]{:S(2)}, u32[]{:S(2)}) collective-permute-start(bf16[2,32,256]{2,1,0:T(8,128)(2,1)} %get-tuple-element.400), channel_id=1, source_target_pairs={{0,8},{1,9},{2,10},{3,11},{4,12},{5,13},{6,14},{7,15},{8,16},{9,17... | collective-permute-start | bytes 98312 | tf_op jit(solution)/shard_map/ppermute | solution.py:20
  287.9 11.5 %collective-permute-start.17 = (bf16[2,32,256]{2,1,0:T(8,128)(2,1)}, bf16[2,32,256]{2,1,0:T(8,128)(2,1)}, u32[]{:S(2)}, u32[]{:S(2)}) collective-permute-start(bf16[2,32,256]{2,1,0:T(8,128)(2,1)} %get-tuple-element.399), channel_id=1, source_target_pairs={{0,7},{1,8},{2,9},{3,10},{4,11},{5,12},{6,13},{7,14},{8,15},{9,16}... | collective-permute-start | bytes 98312 | tf_op jit(solution)/shard_map/ppermute | solution.py:20
  288.7 13.1 %collective-permute-start.18 = (bf16[2,32,256]{2,1,0:T(8,128)(2,1)}, bf16[2,32,256]{2,1,0:T(8,128)(2,1)}, u32[]{:S(2)}, u32[]{:S(2)}) collective-permute-start(bf16[2,32,256]{2,1,0:T(8,128)(2,1)} %get-tuple-element.398), channel_id=1, source_target_pairs={{0,6},{1,7},{2,8},{3,9},{4,10},{5,11},{6,12},{7,13},{8,14},{9,15},... | collective-permute-start | bytes 98312 | tf_op jit(solution)/shard_map/ppermute | solution.py:20
  292.3 10.4 %collective-permute-start.19 = (bf16[2,32,256]{2,1,0:T(8,128)(2,1)}, bf16[2,32,256]{2,1,0:T(8,128)(2,1)}, u32[]{:S(2)}, u32[]{:S(2)}) collective-permute-start(bf16[2,32,256]{2,1,0:T(8,128)(2,1)} %get-tuple-element.397), channel_id=1, source_target_pairs={{0,5},{1,6},{2,7},{3,8},{4,9},{5,10},{6,11},{7,12},{8,13},{9,14},{... | collective-permute-start | bytes 98312 | tf_op jit(solution)/shard_map/ppermute | solution.py:20
  292.3 14.2 %collective-permute-start.20 = (bf16[2,32,256]{2,1,0:T(8,128)(2,1)}, bf16[2,32,256]{2,1,0:T(8,128)(2,1)}, u32[]{:S(2)}, u32[]{:S(2)}) collective-permute-start(bf16[2,32,256]{2,1,0:T(8,128)(2,1)} %get-tuple-element.396), channel_id=1, source_target_pairs={{0,4},{1,5},{2,6},{3,7},{4,8},{5,9},{6,10},{7,11},{8,12},{9,13},{1... | collective-permute-start | bytes 98312 | tf_op jit(solution)/shard_map/ppermute | solution.py:20
  294.6 13.5 %copy-start.59 = (bf16[2,32,256]{2,1,0:T(8,128)(2,1)S(1)}, bf16[2,32,256]{2,1,0:T(8,128)(2,1)}, u32[]{:S(2)}) copy-start(bf16[2,32,256]{2,1,0:T(8,128)(2,1)} %get-tuple-element.390) | copy-start | bytes 98308
  294.6 18.5 %copy-start.58 = (bf16[2,32,256]{2,1,0:T(8,128)(2,1)S(1)}, bf16[2,32,256]{2,1,0:T(8,128)(2,1)}, u32[]{:S(2)}) copy-start(bf16[2,32,256]{2,1,0:T(8,128)(2,1)} %get-tuple-element.389) | copy-start | bytes 98308
  294.6 18.8 %copy-start.57 = (bf16[2,32,256]{2,1,0:T(8,128)(2,1)S(1)}, bf16[2,32,256]{2,1,0:T(8,128)(2,1)}, u32[]{:S(2)}) copy-start(bf16[2,32,256]{2,1,0:T(8,128)(2,1)} %get-tuple-element.388) | copy-start | bytes 98308
  294.6 22.5 %copy-start.56 = (bf16[2,32,256]{2,1,0:T(8,128)(2,1)S(1)}, bf16[2,32,256]{2,1,0:T(8,128)(2,1)}, u32[]{:S(2)}) copy-start(bf16[2,32,256]{2,1,0:T(8,128)(2,1)} %get-tuple-element.387) | copy-start | bytes 98308
  294.6 22.9 %copy-start.55 = (bf16[2,32,256]{2,1,0:T(8,128)(2,1)S(1)}, bf16[2,32,256]{2,1,0:T(8,128)(2,1)}, u32[]{:S(2)}) copy-start(bf16[2,32,256]{2,1,0:T(8,128)(2,1)} %get-tuple-element.401) | copy-start | bytes 98308
  294.6 23.3 %copy-start.54 = (bf16[2,32,256]{2,1,0:T(8,128)(2,1)S(1)}, bf16[2,32,256]{2,1,0:T(8,128)(2,1)}, u32[]{:S(2)}) copy-start(bf16[2,32,256]{2,1,0:T(8,128)(2,1)} %get-tuple-element.386) | copy-start | bytes 98308
  297.1 11.0 %collective-permute-start.21 = (bf16[2,32,256]{2,1,0:T(8,128)(2,1)S(1)}, bf16[2,32,256]{2,1,0:T(8,128)(2,1)S(1)}, u32[]{:S(2)}, u32[]{:S(2)}) collective-permute-start(bf16[2,32,256]{2,1,0:T(8,128)(2,1)S(1)} %copy-done.64), channel_id=1, source_target_pairs={{0,3},{1,4},{2,5},{3,6},{4,7},{5,8},{6,9},{7,10},{8,11},{9,12},{10... | collective-permute-start | bytes 98312 | tf_op jit(solution)/shard_map/ppermute | solution.py:20
  299.4 13.6 %collective-permute-start.22 = (bf16[2,32,256]{2,1,0:T(8,128)(2,1)S(1)}, bf16[2,32,256]{2,1,0:T(8,128)(2,1)S(1)}, u32[]{:S(2)}, u32[]{:S(2)}) collective-permute-start(bf16[2,32,256]{2,1,0:T(8,128)(2,1)S(1)} %copy-done.63), channel_id=1, source_target_pairs={{0,2},{1,3},{2,4},{3,5},{4,6},{5,7},{6,8},{7,9},{8,10},{9,11},{10,... | collective-permute-start | bytes 98312 | tf_op jit(solution)/shard_map/ppermute | solution.py:20
  301.8 11.6 %collective-permute-start.23 = (bf16[2,32,256]{2,1,0:T(8,128)(2,1)S(1)}, bf16[2,32,256]{2,1,0:T(8,128)(2,1)S(1)}, u32[]{:S(2)}, u32[]{:S(2)}) collective-permute-start(bf16[2,32,256]{2,1,0:T(8,128)(2,1)S(1)} %copy-done.62), channel_id=1, source_target_pairs={{0,1},{1,2},{2,3},{3,4},{4,5},{5,6},{6,7},{7,8},{8,9},{9,10},{10,1... | collective-permute-start | bytes 98312 | tf_op jit(solution)/shard_map/ppermute | solution.py:20
  302.7 14.4 %collective-permute-start.24 = (bf16[2,32,256]{2,1,0:T(8,128)(2,1)S(1)}, bf16[2,32,256]{2,1,0:T(8,128)(2,1)S(1)}, u32[]{:S(2)}, u32[]{:S(2)}) collective-permute-start(bf16[2,32,256]{2,1,0:T(8,128)(2,1)S(1)} %copy-done.61), channel_id=1, source_target_pairs={{0,127},{1,0},{2,1},{3,2},{4,3},{5,4},{6,5},{7,6},{8,7},{9,8},{10,... | collective-permute-start | bytes 98312 | tf_op jit(solution)/shard_map/ppermute | solution.py:20
  306.4 11.1 %collective-permute-start.25 = (bf16[2,32,256]{2,1,0:T(8,128)(2,1)S(1)}, bf16[2,32,256]{2,1,0:T(8,128)(2,1)S(1)}, u32[]{:S(2)}, u32[]{:S(2)}) collective-permute-start(bf16[2,32,256]{2,1,0:T(8,128)(2,1)S(1)} %copy-done.60), channel_id=1, source_target_pairs={{0,126},{1,127},{2,0},{3,1},{4,2},{5,3},{6,4},{7,5},{8,6},{9,7},{1... | collective-permute-start | bytes 98312 | tf_op jit(solution)/shard_map/ppermute | solution.py:20
  308.0 9.9 %collective-permute-start.26 = (bf16[2,32,256]{2,1,0:T(8,128)(2,1)S(1)}, bf16[2,32,256]{2,1,0:T(8,128)(2,1)S(1)}, u32[]{:S(2)}, u32[]{:S(2)}) collective-permute-start(bf16[2,32,256]{2,1,0:T(8,128)(2,1)S(1)} %copy-done.59), channel_id=1, source_target_pairs={{0,125},{1,126},{2,127},{3,0},{4,1},{5,2},{6,3},{7,4},{8,5},{9,6},... | collective-permute-start | bytes 98312 | tf_op jit(solution)/shard_map/ppermute | solution.py:20
  313.0 5.4 collective-permute-start.27
  313.4 5.2 collective-permute-start.28
  317.1 5.9 %collective-permute-start.29 = (bf16[2,32,256]{2,1,0:T(8,128)(2,1)S(1)}, bf16[2,32,256]{2,1,0:T(8,128)(2,1)S(1)}, u32[]{:S(2)}, u32[]{:S(2)}) collective-permute-start(bf16[2,32,256]{2,1,0:T(8,128)(2,1)S(1)} %copy-done.56), channel_id=1, source_target_pairs={{0,122},{1,123},{2,124},{3,125},{4,126},{5,127},{6,0},{7,1},{8,2},... | collective-permute-start | bytes 98312 | tf_op jit(solution)/shard_map/ppermute | solution.py:20
  317.5 5.8 collective-permute-start.30
  318.0 5.9 collective-permute-start.31
  324.0 20.8 %copy-start.66 = (pred[2,1024]{1,0:T(4,128)(4,1)S(1)}, pred[2,1024]{1,0:T(4,128)(4,1)}, u32[]{:S(2)}) copy-start(pred[2,1024]{1,0:T(4,128)(4,1)} %get-tuple-element.346) | copy-start | bytes 6148
  (54 other events, 218.7 us)
Sparse Core Ops, SparseCore 0:
  428.8 152.0 all-reduce.2
where the time goes:
time: 604 us; the launch traced here: 593 us
  local copies, waits for them, and re-layouts  203 us (34%)
  waiting for transfers between devices  158 us (26%)
  matrix products  98.2 us (16%)
  other arithmetic  65.2 us (11%)
  starting transfers between devices  52.1 us (9%)
  between operations  15.7 us (3%)
    psum x1, waiting for transfers between devices, per_device(): lax.psum((first_in_grad, first_out_grad, second_in_grad, second_out_grad)...  146 us
    dot_general x56, matrix products, batched(): jnp.einsum(pattern, left_side, right_side, preferred_element_type=jnp.flo...  80.6 us
    ppermute x32, starting transfers between devices, shifted(): return lax.ppermute(value, axis, pairs)  52 us
    unnamed x182, local copies, waits for them, and re-layouts  44.5 us
    gather x1, local copies, waits for them, and re-layouts, per_device(): jnp.take_along_axis(jnp.concatenate([cotangent, arrived[1]], axis=1), pic...  20.9 us
    gather x1, local copies, waits for them, and re-layouts, per_device(): jnp.take_along_axis(jnp.concatenate([rotated_grad, returned], axis=1), pi...  20.8 us
    another operation x5, other arithmetic  17.6 us
    reshape x6, local copies, waits for them, and re-layouts, join_heads(): return grouped.reshape(-1, grouped.shape[3] * grouped.shape[4])  15.9 us
  transfers between devices with their start and end apart: 33, of which 10 were waited for; matrix products, arithmetic and copies ran while one was open for 3% of the time, Pallas kernels for 0%

commit v1 on v0

v1 whole, which is shorter than its diff:
```python
import functools
import math

import jax
import jax.numpy as jnp
from jax import lax
from jax.experimental import pallas as pl
from jax.experimental.pallas import tpu as pltpu
from jax.sharding import PartitionSpec as P

HEADS = 8
BALL = 256
SPAN = 8
CAP = 32
EPSILON = 1e-06
AXES = ("pts", "grp")
OFFSETS = tuple(d for d in range(-SPAN, SPAN + 1) if d != 0)
CLASSES = len(OFFSETS)
SLOTS = CLASSES * CAP
VMEM_LIMIT = 56 * 1024 * 1024

f32 = jnp.float32
bf16 = jnp.bfloat16


def dot(left, right, left_dim=1, right_dim=0):
    return lax.dot_general(
        left, right, (((left_dim,), (right_dim,)), ((), ())), preferred_element_type=f32
    )


def spread_column(row):
    return jnp.transpose(jnp.broadcast_to(row.astype(f32), (128, row.shape[1])))


def one_hot_rows(slot_row, slots):
    ids = lax.broadcasted_iota(jnp.int32, (slots, slot_row.shape[1]), 0)
    return jnp.where(ids == slot_row, 1.0, 0.0).astype(bf16)


def one_hot_picks(pick_column, width):
    lanes = lax.broadcasted_iota(jnp.int32, pick_column.shape, 1).astype(f32)
    pieces = [
        jnp.where(pick_column == lanes + float(128 * piece), 1.0, 0.0).astype(bf16)
        for piece in range(width // 128)
    ]
    return jnp.concatenate(pieces, axis=1)


def place_kernel(own_ref, index_ref, source_ref, cot_ref, meta_ref, *packet_refs, shards):
    samples, rows = index_ref.shape
    own = own_ref[0]
    row_ids = lax.broadcasted_iota(jnp.int32, (rows, 128), 0).astype(f32)
    lane_ids = lax.broadcasted_iota(jnp.int32, (rows, 128), 1).astype(f32)
    shift = rows.bit_length() - 1

    def class_of(ids):
        place = ((ids >> shift) - own + (SPAN + shards)) & (shards - 1)
        return place, jnp.where(place > SPAN, place - 1, place)

    for sample in range(samples):
        index = index_ref[sample : sample + 1, :]
        source = source_ref[sample : sample + 1, :]
        send_place, send_class = class_of(index)
        from_place, from_class = class_of(source)
        place_col = spread_column(send_place)
        source_col = spread_column(source)
        source_f = source.astype(f32)
        floor_f = ((source >> shift) << shift).astype(f32)
        send_rank = []
        receive_rank = []
        for piece in range(rows // 128):
            lanes = slice(128 * piece, 128 * piece + 128)
            here = send_place[:, lanes].astype(f32)
            same = (place_col == here) & (row_ids < lane_ids + float(128 * piece))
            send_rank.append(jnp.sum(jnp.where(same, 1.0, 0.0), axis=0, keepdims=True))
            same = (source_col >= floor_f[:, lanes]) & (source_col < source_f[:, lanes])
            receive_rank.append(jnp.sum(jnp.where(same, 1.0, 0.0), axis=0, keepdims=True))
        send_rank = jnp.concatenate(send_rank, axis=1).astype(jnp.int32)
        receive_rank = jnp.concatenate(receive_rank, axis=1).astype(jnp.int32)
        stays = send_place == SPAN
        home = from_place == SPAN
        send_slot = jnp.where(stays, -1, send_class * CAP + send_rank)
        receive_slot = jnp.where(home, -1, from_class * CAP + receive_rank)
        own_start = own * rows
        meta_ref[sample : sample + 1, :] = send_slot
        meta_ref[2 + sample : 3 + sample, :] = receive_slot
        meta_ref[4 + sample : 5 + sample, :] = jnp.where(
            home, source - own_start, rows + receive_slot
        )
        meta_ref[6 + sample : 7 + sample, :] = jnp.where(
            stays, index - own_start, rows + send_slot
        )
        packed = dot(one_hot_rows(send_slot, SLOTS), cot_ref[sample]).astype(bf16)
        for place in range(CLASSES):
            packet_refs[place][sample] = packed[CAP * place : CAP * place + CAP, :]


def head_masks(shape, axis=1):
    heads = lax.broadcasted_iota(jnp.int32, shape, axis) // (shape[axis] // HEADS)
    return [heads == head for head in range(HEADS)]


def project(rows, inward):
    width = rows.shape[1]
    widened = rows.astype(f32)
    row_scale = lax.rsqrt(jnp.mean(widened * widened, axis=-1, keepdims=True) + EPSILON)
    normed = (widened * row_scale).astype(bf16)
    mixture = dot(normed, inward)
    query_raw = mixture[:, :width]
    key_raw = mixture[:, width : 2 * width]
    value_raw = mixture[:, 2 * width :]
    query_scale = lax.rsqrt(jnp.mean(query_raw * query_raw, axis=-1, keepdims=True) + EPSILON)
    key_scale = lax.rsqrt(jnp.mean(key_raw * key_raw, axis=-1, keepdims=True) + EPSILON)
    return (
        widened,
        row_scale,
        normed,
        query_raw * query_scale,
        query_scale,
        key_raw * key_scale,
        key_scale,
        value_raw,
    )


def masked(array, mask):
    return jnp.where(mask, array, jnp.zeros_like(array))


def forward_kernel(
    nodes_ref, inward_ref, outward_ref, meta_ref, after_ref, attended_ref, *packet_refs
):
    sample, ball = pl.program_id(0), pl.program_id(1)
    width = nodes_ref.shape[2]
    depth = width // HEADS
    widened, _, _, query_unit, _, key_unit, _, value_raw = project(nodes_ref[0], inward_ref[...])
    queries = (query_unit * depth ** (-0.5)).astype(bf16)
    key_rows = key_unit.astype(bf16)
    values_t = jnp.transpose(value_raw).astype(bf16)
    masks = head_masks(key_rows.shape)
    parts = []
    for head in range(HEADS):
        scores = dot(masked(key_rows, masks[head]), queries, 1, 1)
        weights = jnp.exp(scores)
        inverse = 1.0 / jnp.sum(weights, axis=0, keepdims=True)
        prob_low = (weights * inverse).astype(bf16)
        parts.append(dot(values_t[head * depth : (head + 1) * depth, :], prob_low))
    attended_t = jnp.concatenate(parts, axis=0)
    attended_ref[0] = attended_t.astype(bf16)
    attended = jnp.transpose(attended_t).astype(bf16)
    result = (widened + dot(attended, outward_ref[...])).astype(bf16)
    after_ref[0, pl.ds(pl.multiple_of(ball * BALL, BALL), BALL), :] = result

    @pl.when(ball == pl.num_programs(1) - 1)
    def _():
        hits = one_hot_rows(meta_ref[pl.ds(sample, 1), :], SLOTS)
        packed = dot(hits, after_ref[0]).astype(bf16)
        for place in range(CLASSES):
            packet_refs[place][0] = packed[CAP * place : CAP * place + CAP, :]


def attention_backward(
    parts, grad_rows, inward, outward, attended_t, prob_cat, score_cat, grad_stack, query_stack
):
    widened, row_scale, normed, query_unit, query_scale, key_unit, key_scale, value_raw = parts
    width = widened.shape[1]
    depth = width // HEADS
    factor = depth ** (-0.5)
    queries = (query_unit * factor).astype(bf16)
    key_rows = key_unit.astype(bf16)
    values = value_raw.astype(bf16)
    keys_t = jnp.transpose(key_unit).astype(bf16)
    grad_attended = dot(grad_rows, outward, 1, 1).astype(bf16)
    masks = head_masks(key_rows.shape)
    with_forward = attended_t is None
    if with_forward:
        values_t = jnp.transpose(value_raw).astype(bf16)
    outputs = []
    query_parts = []
    for head in range(HEADS):
        block = slice(head * BALL, (head + 1) * BALL)
        band = slice(head * depth, (head + 1) * depth)
        grad_stack[block, :] = masked(grad_attended, masks[head])
        query_stack[block, :] = masked(queries, masks[head])
        scores = dot(masked(key_rows, masks[head]), queries, 1, 1)
        weights = jnp.exp(scores)
        inverse = 1.0 / jnp.sum(weights, axis=0, keepdims=True)
        prob_full = weights * inverse
        prob_low = prob_full.astype(bf16)
        prob_cat[:, block] = prob_low
        if with_forward:
            outputs.append(dot(values_t[band, :], prob_low))
        grad_probs = dot(masked(values, masks[head]), grad_attended, 1, 1)
        column_sum = jnp.sum(grad_probs * prob_full, axis=0, keepdims=True)
        grad_scores = (prob_full * (grad_probs - column_sum)).astype(bf16)
        score_cat[:, block] = grad_scores
        query_parts.append(dot(keys_t[band, :], grad_scores))
    if with_forward:
        attended_t = jnp.concatenate(outputs, axis=0).astype(bf16)
    grad_outward = dot(attended_t, grad_rows)
    grad_queries = jnp.transpose(jnp.concatenate(query_parts, axis=0)) * factor
    grad_values = dot(prob_cat[...], grad_stack[...])
    grad_keys = dot(score_cat[...], query_stack[...])
    grad_qraw = query_scale * (
        grad_queries - query_unit * jnp.mean(grad_queries * query_unit, axis=-1, keepdims=True)
    )
    grad_kraw = key_scale * (
        grad_keys - key_unit * jnp.mean(grad_keys * key_unit, axis=-1, keepdims=True)
    )
    grad_mixture = jnp.concatenate([grad_qraw, grad_kraw, grad_values], axis=1).astype(bf16)
    grad_inward = dot(normed, grad_mixture, 0, 0)
    grad_normed = dot(grad_mixture, inward, 1, 1)
    unit_rows = widened * row_scale
    grad_input = grad_rows.astype(f32) + row_scale * (
        grad_normed - unit_rows * jnp.mean(grad_normed * unit_rows, axis=-1, keepdims=True)
    )
    return grad_input.astype(bf16), grad_inward, grad_outward


def add_up(first, total_ref, term):
    @pl.when(first)
    def _():
        total_ref[...] = term

    @pl.when(jnp.logical_not(first))
    def _():
        total_ref[...] += term


def second_kernel(*refs):
    meta_ref, after_ref, cot_ref, inward_ref, outward_ref = refs[:5]
    arrived_refs = refs[5 : 5 + CLASSES]
    cot_refs = refs[5 + CLASSES : 5 + 2 * CLASSES]
    outs = refs[5 + 2 * CLASSES :]
    grad_ref, inward_grad_ref, outward_grad_ref = outs[:3]
    packet_refs = outs[3 : 3 + CLASSES]
    (picks, landed, landed_cot, prob_cat, score_cat, grad_stack, query_stack) = outs[3 + CLASSES :]
    sample, ball = pl.program_id(0), pl.program_id(1)
    rows = after_ref.shape[1]

    @pl.when(ball == 0)
    def _():
        picks[...] = spread_column(meta_ref[pl.ds(4 + sample, 1), :])
        for place in range(CLASSES):
            landed[CAP * place : CAP * place + CAP, :] = arrived_refs[place][0]
            landed_cot[CAP * place : CAP * place + CAP, :] = cot_refs[place][0]

    here = pl.ds(pl.multiple_of(ball * BALL, BALL), BALL)
    hits = one_hot_picks(picks[here, :], rows + SLOTS)
    rotated = (dot(hits[:, :rows], after_ref[0]) + dot(hits[:, rows:], landed[...])).astype(bf16)
    rotated_cot = (
        dot(hits[:, :rows], cot_ref[0]) + dot(hits[:, rows:], landed_cot[...])
    ).astype(bf16)
    grad_input, grad_inward, grad_outward = attention_backward(
        project(rotated, inward_ref[...]),
        rotated_cot,
        inward_ref[...],
        outward_ref[...],
        None,
        prob_cat,
        score_cat,
        grad_stack,
        query_stack,
    )
    grad_ref[0, here, :] = grad_input
    first = (sample == 0) & (ball == 0)
    add_up(first, inward_grad_ref, grad_inward)
    add_up(first, outward_grad_ref, grad_outward)

    @pl.when(ball == pl.num_programs(1) - 1)
    def _():
        hits = one_hot_rows(meta_ref[pl.ds(2 + sample, 1), :], SLOTS)
        packed = dot(hits, grad_ref[0]).astype(bf16)
        for place in range(CLASSES):
            packet_refs[place][0] = packed[CAP * place : CAP * place + CAP, :]


def first_kernel(*refs):
    meta_ref, nodes_ref, rotated_ref, attended_ref, inward_ref, outward_ref = refs[:6]
    returned_refs = refs[6 : 6 + CLASSES]
    outs = refs[6 + CLASSES :]
    grad_ref, inward_grad_ref, outward_grad_ref = outs[:3]
    (picks, landed, prob_cat, score_cat, grad_stack, query_stack) = outs[3:]
    sample, ball = pl.program_id(0), pl.program_id(1)
    rows = rotated_ref.shape[1]

    @pl.when(ball == 0)
    def _():
        picks[...] = spread_column(meta_ref[pl.ds(6 + sample, 1), :])
        for place in range(CLASSES):
            landed[CAP * place : CAP * place + CAP, :] = returned_refs[place][0]

    here = pl.ds(pl.multiple_of(ball * BALL, BALL), BALL)
    hits = one_hot_picks(picks[here, :], rows + SLOTS)
    grad_after = (
        dot(hits[:, :rows], rotated_ref[0]) + dot(hits[:, rows:], landed[...])
    ).astype(bf16)
    grad_input, grad_inward, grad_outward = attention_backward(
        project(nodes_ref[0], inward_ref[...]),
        grad_after,
        inward_ref[...],
        outward_ref[...],
        attended_ref[0],
        prob_cat,
        score_cat,
        grad_stack,
        query_stack,
    )
    grad_ref[0] = grad_input
    first = (sample == 0) & (ball == 0)
    add_up(first, inward_grad_ref, grad_inward)
    add_up(first, outward_grad_ref, grad_outward)


def shifted(value, steps):
    count = lax.axis_size(AXES)
    pairs = [(source, (source + steps) % count) for source in range(count)]
    return lax.ppermute(value, AXES, pairs)


def exchange(packets):
    return [shifted(packets[CLASSES - 1 - place], -OFFSETS[place]) for place in range(CLASSES)]


def reduce_all(parts):
    count = lax.axis_size(AXES)
    flat = jnp.concatenate([part.reshape(-1, 256) for part in parts], axis=0)
    pieces = flat.astype(bf16).reshape(count, -1, 256)
    mine = lax.all_to_all(pieces, AXES, 0, 0, tiled=True)
    total = jnp.sum(mine.astype(f32), axis=0).astype(bf16)
    spread = jnp.broadcast_to(total[None], pieces.shape)
    whole = lax.all_to_all(spread, AXES, 0, 0, tiled=True)
    return whole.reshape(flat.shape)


def per_device(
    nodes,
    cotangent,
    first_inward,
    first_outward,
    second_inward,
    second_outward,
    rotated_source,
    rotated_index,
):
    samples, rows, width = nodes.shape
    shards = lax.axis_size(AXES)
    own = lax.axis_index(AXES).astype(jnp.int32).reshape(1)
    balls = rows // BALL
    params = pltpu.CompilerParams(vmem_limit_bytes=VMEM_LIMIT)
    packet_shape = jax.ShapeDtypeStruct((samples, CAP, width), bf16)
    whole = lambda *shape: pl.BlockSpec(shape, lambda s, b: (0,) * len(shape))
    per_sample = lambda n: pl.BlockSpec((1, n, width), lambda s, b: (s, 0, 0))
    per_ball = pl.BlockSpec((1, BALL, width), lambda s, b: (s, b, 0))
    row_shape = jax.ShapeDtypeStruct((samples, rows, width), bf16)
    grad_shapes = [
        jax.ShapeDtypeStruct((width, 3 * width), f32),
        jax.ShapeDtypeStruct((width, width), f32),
    ]
    grad_specs = [whole(width, 3 * width), whole(width, width)]
    weight_specs = [whole(width, 3 * width), whole(width, width)]
    meta_spec = whole(8, rows)
    attention_scratch = [
        pltpu.VMEM((BALL, HEADS * BALL), bf16),
        pltpu.VMEM((BALL, HEADS * BALL), bf16),
        pltpu.VMEM((HEADS * BALL, width), bf16),
        pltpu.VMEM((HEADS * BALL, width), bf16),
    ]
    vmem = pl.BlockSpec(memory_space=pltpu.VMEM)
    meta, *cot_packets = pl.pallas_call(
        functools.partial(place_kernel, shards=shards),
        name="place",
        in_specs=[pl.BlockSpec(memory_space=pltpu.SMEM), vmem, vmem, vmem],
        out_specs=[vmem] * (1 + CLASSES),
        out_shape=[jax.ShapeDtypeStruct((8, rows), jnp.int32)] + [packet_shape] * CLASSES,
        compiler_params=params,
    )(own, rotated_index, rotated_source, cotangent)
    cot_arrived = exchange(cot_packets)
    after_first, attended_t, *packets = pl.pallas_call(
        forward_kernel,
        name="forward",
        grid=(samples, balls),
        in_specs=[per_ball] + weight_specs + [meta_spec],
        out_specs=[per_sample(rows), per_ball] + [per_sample(CAP)] * CLASSES,
        out_shape=[row_shape, row_shape] + [packet_shape] * CLASSES,
        compiler_params=params,
    )(nodes, first_inward, first_outward, meta)
    arrived = exchange(packets)
    rotated_grad, second_in_grad, second_out_grad, *back_packets = pl.pallas_call(
        second_kernel,
        name="second",
        grid=(samples, balls),
        in_specs=[meta_spec, per_sample(rows), per_sample(rows)]
        + weight_specs
        + [per_sample(CAP)] * (2 * CLASSES),
        out_specs=[per_sample(rows)] + grad_specs + [per_sample(CAP)] * CLASSES,
        out_shape=[row_shape] + grad_shapes + [packet_shape] * CLASSES,
        scratch_shapes=[
            pltpu.VMEM((rows, 128), f32),
            pltpu.VMEM((SLOTS, width), bf16),
            pltpu.VMEM((SLOTS, width), bf16),
        ]
        + attention_scratch,
        compiler_params=params,
    )(meta, after_first, cotangent, second_inward, second_outward, *arrived, *cot_arrived)
    returned = exchange(back_packets)
    input_grad, first_in_grad, first_out_grad = pl.pallas_call(
        first_kernel,
        name="first",
        grid=(samples, balls),
        in_specs=[meta_spec, per_ball, per_sample(rows), per_ball]
        + weight_specs
        + [per_sample(CAP)] * CLASSES,
        out_specs=[per_ball] + grad_specs,
        out_shape=[row_shape] + grad_shapes,
        scratch_shapes=[pltpu.VMEM((rows, 128), f32), pltpu.VMEM((SLOTS, width), bf16)]
        + attention_scratch,
        compiler_params=params,
    )(meta, nodes, rotated_grad, attended_t, first_inward, first_outward, *returned)
    factor = 1.0 / math.sqrt(samples * rows * shards)
    terms = [first_in_grad, first_out_grad, second_in_grad, second_out_grad]
    summed = reduce_all(terms)
    results = []
    start = 0
    for term in terms:
        length = term.size // 256
        results.append(summed[start : start + length].reshape(term.shape).astype(f32) * factor)
        start += length
    return (input_grad, *results)


def solution(mesh):
    in_specs = (
        P(None, AXES, None),
        P(None, AXES, None),
        P(),
        P(),
        P(),
        P(),
        P(None, AXES),
        P(None, AXES),
    )
    out_specs = (P(None, AXES, None), P(), P(), P(), P())
    return jax.shard_map(
        per_device, mesh=mesh, in_specs=in_specs, out_specs=out_specs, check_vma=False
    )
```

time: 604 us -> 280 us (0.46); the launches traced: 593 us -> 275 us
  local copies, waits for them, and re-layouts: 203 us -> 3.75 us
  waiting for transfers between devices: 158 us -> 17 us
  Pallas kernels: 0 us -> 114 us
  matrix products: 98.2 us -> 0 us
  other arithmetic: 65.2 us -> 5.63 us
  blocking collectives: 0 us -> 50.6 us
  starting transfers between devices: 52.1 us -> 82.8 us
  between operations: 15.7 us -> 1.51 us
    psum x1 -> x0, waiting for transfers between devices: 146 us -> none  [per_device(): lax.psum((first_in_grad, first_out_grad, second_in_grad, second_out_grad)...]
    pallas_call x0 -> x4, Pallas kernels: none -> 114 us  [the longest x1 47.4 us: per_device(): pl.pallas_call(second_kernel, name='second', grid=(samples, balls), in_sp...]
    dot_general x67 -> x0, matrix products: 98.2 us -> none  [the longest x56 80.6 us: batched(): jnp.einsum(pattern, left_side, right_side, preferred_element_type=jnp.flo...]
    gather x3 -> x0, local copies, waits for them, and re-layouts: 52.8 us -> none  [the longest x1 20.9 us: per_device(): jnp.take_along_axis(jnp.concatenate([cotangent, arrived[1]], axis=1), pic...]
    all_to_all x0 -> x2, blocking collectives: none -> 50.6 us  [the longest x1 27.6 us: reduce_all(): mine = lax.all_to_all(pieces, AXES, 0, 0, tiled=True)]
    unnamed x182 -> x104, local copies, waits for them, and re-layouts: 44.5 us -> 1.1 us
    ppermute x32 -> x48, starting transfers between devices: 52 us -> 82.8 us  [shifted(): return lax.ppermute(value, AXES, pairs)]
    reshape x14 -> x2, local copies, waits for them, and re-layouts: 28.5 us -> 0.37 us  [reduce_all(): flat = jnp.concatenate([part.reshape(-1, 256) for part in parts], axis=0)]
  transfers between devices with their start and end apart: 33 -> 48, of which waited for: 10 -> 11; matrix products, arithmetic and copies ran while one was open for 3% -> 1% of each run, Pallas kernels for 0% -> 8%
where the time goes in v1:
time: 280 us; the launch traced here: 275 us
  Pallas kernels  114 us (41%)
  starting transfers between devices  82.8 us (30%)
  blocking collectives  50.6 us (18%)
  waiting for transfers between devices  17 us (6%)
  other arithmetic  5.63 us (2%)
  local copies, waits for them, and re-layouts  3.75 us (1%)
    ppermute x48, starting transfers between devices, shifted(): return lax.ppermute(value, AXES, pairs)  82.8 us
    pallas_call x1, Pallas kernels, per_device(): pl.pallas_call(second_kernel, name='second', grid=(samples, balls), in_sp...  47.4 us
    pallas_call x1, Pallas kernels, per_device(): pl.pallas_call(first_kernel, name='first', grid=(samples, balls), in_spec...  40.9 us
    all_to_all x1, blocking collectives, reduce_all(): mine = lax.all_to_all(pieces, AXES, 0, 0, tiled=True)  27.6 us
    all_to_all x1, blocking collectives, reduce_all(): whole = lax.all_to_all(spread, AXES, 0, 0, tiled=True)  23 us
    pallas_call x1, Pallas kernels, per_device(): pl.pallas_call(forward_kernel, name='forward', grid=(samples, balls), in_...  20.9 us
    ppermute x48, waiting for transfers between devices, shifted(): return lax.ppermute(value, AXES, pairs)  17 us
  transfers between devices with their start and end apart: 48, of which 11 were waited for; matrix products, arithmetic and copies ran while one was open for 1% of the time, Pallas kernels for 8%

profile of v1, /device:TPU:1, one launch (start us, length us, event | category | flops | bytes accessed | tf_op | source)
XLA Modules:
  0.0 275.5 jit_solution(1485867175618909606)
XLA Ops:
  0.6 5.1 %place.1 = (s32[8,1024]{1,0:T(8,128)}, bf16[2,32,256]{2,1,0:T(8,128)(2,1)}, bf16[2,32,256]{2,1,0:T(8,128)(2,1)}, bf16[2,32,256]{2,1,0:T(8,128)(2,1)}, bf16[2,32,...) custom-call(s32[1]{0:T(128)} %bitcast.own_ref, ...), custom_call_target="tpu_custom_call" | custom-call | tf_op jit(solution)/shard_map/place/pallas_call | solution.py:371
  5.7 2.2 collective-permute-start.16
  7.9 4.3 %collective-permute-start.17 = (bf16[2,32,256]{2,1,0:T(8,128)(2,1)}, bf16[2,32,256]{2,1,0:T(8,128)(2,1)S(1)}, u32[]{:S(2)}, u32[]{:S(2)}) collective-permute-start(bf16[2,32,256]{2,1,0:T(8,128)(2,1)} %get-tuple-element.81), channel_id=1, source_target_pairs={{0,7},{1,8},{2,9},{3,10},{4,11},{5,12},{6,13},{7,14},{8,15},{9,16}... | collective-permute-start | bytes 98312 | tf_op jit(solution)/shard_map/ppermute | solution.py:319
  12.3 1.5 collective-permute-start.18
  13.8 2.2 collective-permute-start.20
  16.0 1.6 collective-permute-start.21
  17.6 1.2 collective-permute-start.22
  18.8 2.2 collective-permute-done.18.refs_23_
  21.0 1.2 collective-permute-done.19.refs_24_
  22.2 1.8 collective-permute-start.24
  24.4 4.0 %collective-permute-start.26 = (bf16[2,32,256]{2,1,0:T(8,128)(2,1)}, bf16[2,32,256]{2,1,0:T(8,128)(2,1)S(1)}, u32[]{:S(2)}, u32[]{:S(2)}) collective-permute-start(bf16[2,32,256]{2,1,0:T(8,128)(2,1)} %get-tuple-element.90), channel_id=1, source_target_pairs={{0,125},{1,126},{2,127},{3,0},{4,1},{5,2},{6,3},{7,4},{8,5},{9,6},... | collective-permute-start | bytes 98312 | tf_op jit(solution)/shard_map/ppermute | solution.py:319
  28.4 20.9 %forward.1 = (bf16[2,1024,256]{2,1,0:T(8,128)(2,1)}, bf16[2,1024,256]{2,1,0:T(8,128)(2,1)}, bf16[2,32,256]{2,1,0:T(8,128)(2,1)}, bf16[2,32,256]{2,1,0:T(8,128)(2...) custom-call(bf16[2,1024,256]{2,1,0:T(8,128)(2,1)} %refs_1_.1, ...), custom_call_target="tpu_custom_call" | custom-call | tf_op jit(solution)/shard_map/forward/pallas_call | solution.py:380
  49.4 1.7 collective-permute-start.28
  51.1 2.7 collective-permute-start.29
  54.0 1.5 collective-permute-start.31
  55.8 4.4 %collective-permute-start.1 = (bf16[2,32,256]{2,1,0:T(8,128)(2,1)}, bf16[2,32,256]{2,1,0:T(8,128)(2,1)S(1)}, u32[]{:S(2)}, u32[]{:S(2)}) collective-permute-start(bf16[2,32,256]{2,1,0:T(8,128)(2,1)} %get-tuple-element.65), channel_id=1, source_target_pairs={{0,7},{1,8},{2,9},{3,10},{4,11},{5,12},{6,13},{7,14},{8,15},{9,16}... | collective-permute-start | bytes 98312 | tf_op jit(solution)/shard_map/ppermute | solution.py:319
  60.1 1.3 collective-permute-start.2
  61.5 3.2 %collective-permute-start.4 = (bf16[2,32,256]{2,1,0:T(8,128)(2,1)}, bf16[2,32,256]{2,1,0:T(8,128)(2,1)S(1)}, u32[]{:S(2)}, u32[]{:S(2)}) collective-permute-start(bf16[2,32,256]{2,1,0:T(8,128)(2,1)} %get-tuple-element.68), channel_id=1, source_target_pairs={{0,4},{1,5},{2,6},{3,7},{4,8},{5,9},{6,10},{7,11},{8,12},{9,13},{1... | collective-permute-start | bytes 98312 | tf_op jit(solution)/shard_map/ppermute | solution.py:319
  64.6 2.7 collective-permute-start.5
  67.3 1.8 collective-permute-start.6
  69.8 2.3 collective-permute-start.8
  72.1 1.8 collective-permute-start.9
  74.0 4.0 %collective-permute-start.10 = (bf16[2,32,256]{2,1,0:T(8,128)(2,1)}, bf16[2,32,256]{2,1,0:T(8,128)(2,1)S(1)}, u32[]{:S(2)}, u32[]{:S(2)}) collective-permute-start(bf16[2,32,256]{2,1,0:T(8,128)(2,1)} %get-tuple-element.74), channel_id=1, source_target_pairs={{0,125},{1,126},{2,127},{3,0},{4,1},{5,2},{6,3},{7,4},{8,5},{9,6},... | collective-permute-start | bytes 98312 | tf_op jit(solution)/shard_map/ppermute | solution.py:319
  79.0 1.9 collective-permute-start.13
  80.8 1.9 collective-permute-start.15
  83.5 1.6 collective-permute-done.13.refs_18_
  85.1 1.4 collective-permute-done.14.refs_19_
  86.6 2.7 collective-permute-done.15.refs_20_
  89.9 47.4 %second.1 = (bf16[2,1024,256]{2,1,0:T(8,128)(2,1)}, f32[256,768]{1,0:T(8,128)}, f32[256,256]{1,0:T(8,128)}, bf16[2,32,256]{2,1,0:T(8,128)(2,1)}, bf16[2,32,256]{...) custom-call(s32[8,1024]{1,0:T(8,128)} %get-tuple-element.62.meta_ref, ...), custom_call_target="tpu_custom_call" | custom-call | tf_op jit(solution)/shard_map/second/pallas_call | solution.py:390
  137.3 11.3 %collective-permute-start.32 = (bf16[2,32,256]{2,1,0:T(8,128)(2,1)}, bf16[2,32,256]{2,1,0:T(8,128)(2,1)S(1)}, u32[]{:S(2)}, u32[]{:S(2)}) collective-permute-start(bf16[2,32,256]{2,1,0:T(8,128)(2,1)} %get-tuple-element.98), channel_id=1, source_target_pairs={{0,8},{1,9},{2,10},{3,11},{4,12},{5,13},{6,14},{7,15},{8,16},{9,17... | collective-permute-start | bytes 98312 | tf_op jit(solution)/shard_map/ppermute | solution.py:319
  149.4 4.4 %collective-permute-start.34 = (bf16[2,32,256]{2,1,0:T(8,128)(2,1)}, bf16[2,32,256]{2,1,0:T(8,128)(2,1)S(1)}, u32[]{:S(2)}, u32[]{:S(2)}) collective-permute-start(bf16[2,32,256]{2,1,0:T(8,128)(2,1)} %get-tuple-element.100), channel_id=1, source_target_pairs={{0,6},{1,7},{2,8},{3,9},{4,10},{5,11},{6,12},{7,13},{8,14},{9,15},... | collective-permute-start | bytes 98312 | tf_op jit(solution)/shard_map/ppermute | solution.py:319
  154.0 2.1 collective-permute-start.37
  156.1 1.1 collective-permute-start.38
  157.2 0.9 collective-permute-done.34.refs_8_
  159.0 3.2 %collective-permute-done.35.refs_9_ = bf16[2,32,256]{2,1,0:T(8,128)(2,1)S(1)} collective-permute-done((bf16[2,32,256]{2,1,0:T(8,128)(2,1)}, bf16[2,32,256]{2,1,0:T(8,128)(2,1)S(1)}, u32[]{:S(2)}, u32[]{:S(2)}) %collective-permute-start.35) | collective-permute-done | bytes 32800 | tf_op jit(solution)/shard_map/ppermute | solution.py:319
  162.4 3.5 %collective-permute-start.42 = (bf16[2,32,256]{2,1,0:T(8,128)(2,1)}, bf16[2,32,256]{2,1,0:T(8,128)(2,1)S(1)}, u32[]{:S(2)}, u32[]{:S(2)}) collective-permute-start(bf16[2,32,256]{2,1,0:T(8,128)(2,1)} %get-tuple-element.108), channel_id=1, source_target_pairs={{0,125},{1,126},{2,127},{3,0},{4,1},{5,2},{6,3},{7,4},{8,5},{9,6},... | collective-permute-start | bytes 98312 | tf_op jit(solution)/shard_map/ppermute | solution.py:319
  166.6 3.6 %collective-permute-start.44 = (bf16[2,32,256]{2,1,0:T(8,128)(2,1)}, bf16[2,32,256]{2,1,0:T(8,128)(2,1)S(1)}, u32[]{:S(2)}, u32[]{:S(2)}) collective-permute-start(bf16[2,32,256]{2,1,0:T(8,128)(2,1)} %get-tuple-element.110), channel_id=1, source_target_pairs={{0,123},{1,124},{2,125},{3,126},{4,127},{5,0},{6,1},{7,2},{8,3},{9... | collective-permute-start | bytes 98312 | tf_op jit(solution)/shard_map/ppermute | solution.py:319
  170.2 2.3 collective-permute-start.46
  172.5 1.0 convert.18
  173.5 1.2 convert.17
  175.0 1.5 collective-permute-done.45.refs_19_
  177.8 40.9 %first.1 = (bf16[2,1024,256]{2,1,0:T(8,128)(2,1)}, f32[256,768]{1,0:T(8,128)}, f32[256,256]{1,0:T(8,128)}) custom-call(s32[8,1024]{1,0:T(8,128)} %get-tuple-element.62.meta_ref.refs_0_, bf16[2,1024,256]{2,1,0:T(8,128)(2,1)} %refs_1_.1, bf16[2,1024,256]{2,1,0:T(8,128)(2,1)} %get-tuple-element.96.refs_2_, bf16[2,1024,256]{2,1,0:T(8,128)(2,1)} %get-tuple-element.97.refs_3_, ...), custom_call_target="tpu_custom_call" | custom-call | tf_op jit(solution)/shard_map/first/pallas_call | solution.py:408
  218.7 1.0 convert.16
  219.7 1.2 convert.15
  221.1 27.6 %all_to_all.10 = bf16[128,16,256]{2,1,0:T(8,128)(2,1)S(1)} all-to-all(bf16[128,16,256]{2,1,0:T(8,128)(2,1)S(1)} %bitcast.4), channel_id=1, replica_groups=mesh['pts'=32,'grp'=4] {'pts','grp'}, dimensions={0} | all-to-all | bytes 2097152 | tf_op jit(solution)/shard_map/all_to_all | solution.py:330
  249.0 23.0 %all_to_all.11 = bf16[128,16,256]{2,1,0:T(8,128)(2,1)S(1)} all-to-all(bf16[128,16,256]{2,1,0:T(8,128)(2,1)S(1)} %broadcast_in_dim.2), channel_id=1, replica_groups=mesh['pts'=32,'grp'=4] {'pts','grp'}, dimensions={0} | all-to-all | bytes 2097152 | tf_op jit(solution)/shard_map/all_to_all | solution.py:333
  272.2 1.1 mul.33
  273.4 1.1 mul.29
  (171 shorter events, 9.6 us)
Async XLA Ops:
  5.7 10.2 %collective-permute-start.16 = (bf16[2,32,256]{2,1,0:T(8,128)(2,1)}, bf16[2,32,256]{2,1,0:T(8,128)(2,1)S(1)}, u32[]{:S(2)}, u32[]{:S(2)}) collective-permute-start(bf16[2,32,256]{2,1,0:T(8,128)(2,1)} %get-tuple-element.80), channel_id=1, source_target_pairs={{0,8},{1,9},{2,10},{3,11},{4,12},{5,13},{6,14},{7,15},{8,16},{9,17... | collective-permute-start | bytes 98312 | tf_op jit(solution)/shard_map/ppermute | solution.py:319
  7.9 9.6 %collective-permute-start.17 = (bf16[2,32,256]{2,1,0:T(8,128)(2,1)}, bf16[2,32,256]{2,1,0:T(8,128)(2,1)S(1)}, u32[]{:S(2)}, u32[]{:S(2)}) collective-permute-start(bf16[2,32,256]{2,1,0:T(8,128)(2,1)} %get-tuple-element.81), channel_id=1, source_target_pairs={{0,7},{1,8},{2,9},{3,10},{4,11},{5,12},{6,13},{7,14},{8,15},{9,16}... | collective-permute-start | bytes 98312 | tf_op jit(solution)/shard_map/ppermute | solution.py:319
  12.3 8.7 %collective-permute-start.18 = (bf16[2,32,256]{2,1,0:T(8,128)(2,1)}, bf16[2,32,256]{2,1,0:T(8,128)(2,1)S(1)}, u32[]{:S(2)}, u32[]{:S(2)}) collective-permute-start(bf16[2,32,256]{2,1,0:T(8,128)(2,1)} %get-tuple-element.82), channel_id=1, source_target_pairs={{0,6},{1,7},{2,8},{3,9},{4,10},{5,11},{6,12},{7,13},{8,14},{9,15},... | collective-permute-start | bytes 98312 | tf_op jit(solution)/shard_map/ppermute | solution.py:319
  13.8 8.4 %collective-permute-start.19 = (bf16[2,32,256]{2,1,0:T(8,128)(2,1)}, bf16[2,32,256]{2,1,0:T(8,128)(2,1)S(1)}, u32[]{:S(2)}, u32[]{:S(2)}) collective-permute-start(bf16[2,32,256]{2,1,0:T(8,128)(2,1)} %get-tuple-element.83), channel_id=1, source_target_pairs={{0,5},{1,6},{2,7},{3,8},{4,9},{5,10},{6,11},{7,12},{8,13},{9,14},{... | collective-permute-start | bytes 98312 | tf_op jit(solution)/shard_map/ppermute | solution.py:319
  13.8 10.2 %collective-permute-start.20 = (bf16[2,32,256]{2,1,0:T(8,128)(2,1)}, bf16[2,32,256]{2,1,0:T(8,128)(2,1)S(1)}, u32[]{:S(2)}, u32[]{:S(2)}) collective-permute-start(bf16[2,32,256]{2,1,0:T(8,128)(2,1)} %get-tuple-element.84), channel_id=1, source_target_pairs={{0,4},{1,5},{2,6},{3,7},{4,8},{5,9},{6,10},{7,11},{8,12},{9,13},{1... | collective-permute-start | bytes 98312 | tf_op jit(solution)/shard_map/ppermute | solution.py:319
  16.0 8.4 %collective-permute-start.21 = (bf16[2,32,256]{2,1,0:T(8,128)(2,1)}, bf16[2,32,256]{2,1,0:T(8,128)(2,1)S(1)}, u32[]{:S(2)}, u32[]{:S(2)}) collective-permute-start(bf16[2,32,256]{2,1,0:T(8,128)(2,1)} %get-tuple-element.85), channel_id=1, source_target_pairs={{0,3},{1,4},{2,5},{3,6},{4,7},{5,8},{6,9},{7,10},{8,11},{9,12},{10... | collective-permute-start | bytes 98312 | tf_op jit(solution)/shard_map/ppermute | solution.py:319
  17.6 10.8 %collective-permute-start.22 = (bf16[2,32,256]{2,1,0:T(8,128)(2,1)}, bf16[2,32,256]{2,1,0:T(8,128)(2,1)S(1)}, u32[]{:S(2)}, u32[]{:S(2)}) collective-permute-start(bf16[2,32,256]{2,1,0:T(8,128)(2,1)} %get-tuple-element.86), channel_id=1, source_target_pairs={{0,2},{1,3},{2,4},{3,5},{4,6},{5,7},{6,8},{7,9},{8,10},{9,11},{10,... | collective-permute-start | bytes 98312 | tf_op jit(solution)/shard_map/ppermute | solution.py:319
  21.0 28.3 %collective-permute-start.23 = (bf16[2,32,256]{2,1,0:T(8,128)(2,1)}, bf16[2,32,256]{2,1,0:T(8,128)(2,1)S(1)}, u32[]{:S(2)}, u32[]{:S(2)}) collective-permute-start(bf16[2,32,256]{2,1,0:T(8,128)(2,1)} %get-tuple-element.87), channel_id=1, source_target_pairs={{0,1},{1,2},{2,3},{3,4},{4,5},{5,6},{6,7},{7,8},{8,9},{9,10},{10,1... | collective-permute-start | bytes 98312 | tf_op jit(solution)/shard_map/ppermute | solution.py:319
  22.2 28.9 %collective-permute-start.24 = (bf16[2,32,256]{2,1,0:T(8,128)(2,1)}, bf16[2,32,256]{2,1,0:T(8,128)(2,1)S(1)}, u32[]{:S(2)}, u32[]{:S(2)}) collective-permute-start(bf16[2,32,256]{2,1,0:T(8,128)(2,1)} %get-tuple-element.88), channel_id=1, source_target_pairs={{0,127},{1,0},{2,1},{3,2},{4,3},{5,4},{6,5},{7,6},{8,7},{9,8},{10,... | collective-permute-start | bytes 98312 | tf_op jit(solution)/shard_map/ppermute | solution.py:319
  24.0 29.9 %collective-permute-start.25 = (bf16[2,32,256]{2,1,0:T(8,128)(2,1)}, bf16[2,32,256]{2,1,0:T(8,128)(2,1)S(1)}, u32[]{:S(2)}, u32[]{:S(2)}) collective-permute-start(bf16[2,32,256]{2,1,0:T(8,128)(2,1)} %get-tuple-element.89), channel_id=1, source_target_pairs={{0,126},{1,127},{2,0},{3,1},{4,2},{5,3},{6,4},{7,5},{8,6},{9,7},{1... | collective-permute-start | bytes 98312 | tf_op jit(solution)/shard_map/ppermute | solution.py:319
  24.4 29.5 %collective-permute-start.26 = (bf16[2,32,256]{2,1,0:T(8,128)(2,1)}, bf16[2,32,256]{2,1,0:T(8,128)(2,1)S(1)}, u32[]{:S(2)}, u32[]{:S(2)}) collective-permute-start(bf16[2,32,256]{2,1,0:T(8,128)(2,1)} %get-tuple-element.90), channel_id=1, source_target_pairs={{0,125},{1,126},{2,127},{3,0},{4,1},{5,2},{6,3},{7,4},{8,5},{9,6},... | collective-permute-start | bytes 98312 | tf_op jit(solution)/shard_map/ppermute | solution.py:319
  28.4 27.0 %collective-permute-start.27 = (bf16[2,32,256]{2,1,0:T(8,128)(2,1)}, bf16[2,32,256]{2,1,0:T(8,128)(2,1)S(1)}, u32[]{:S(2)}, u32[]{:S(2)}) collective-permute-start(bf16[2,32,256]{2,1,0:T(8,128)(2,1)} %get-tuple-element.91), channel_id=1, source_target_pairs={{0,124},{1,125},{2,126},{3,127},{4,0},{5,1},{6,2},{7,3},{8,4},{9,5... | collective-permute-start | bytes 98312 | tf_op jit(solution)/shard_map/ppermute | solution.py:319
  49.4 6.4 %collective-permute-start.28 = (bf16[2,32,256]{2,1,0:T(8,128)(2,1)S(1)}, bf16[2,32,256]{2,1,0:T(8,128)(2,1)S(1)}, u32[]{:S(2)}, u32[]{:S(2)}) collective-permute-start(bf16[2,32,256]{2,1,0:T(8,128)(2,1)S(1)} %copy-done.51), channel_id=1, source_target_pairs={{0,123},{1,124},{2,125},{3,126},{4,127},{5,0},{6,1},{7,2},{8,3},{9... | collective-permute-start | bytes 98312 | tf_op jit(solution)/shard_map/ppermute | solution.py:319
  51.1 9.0 %collective-permute-start.29 = (bf16[2,32,256]{2,1,0:T(8,128)(2,1)S(1)}, bf16[2,32,256]{2,1,0:T(8,128)(2,1)S(1)}, u32[]{:S(2)}, u32[]{:S(2)}) collective-permute-start(bf16[2,32,256]{2,1,0:T(8,128)(2,1)S(1)} %copy-done.50), channel_id=1, source_target_pairs={{0,122},{1,123},{2,124},{3,125},{4,126},{5,127},{6,0},{7,1},{8,2},... | collective-permute-start | bytes 98312 | tf_op jit(solution)/shard_map/ppermute | solution.py:319
  53.8 7.6 %collective-permute-start.30 = (bf16[2,32,256]{2,1,0:T(8,128)(2,1)S(1)}, bf16[2,32,256]{2,1,0:T(8,128)(2,1)S(1)}, u32[]{:S(2)}, u32[]{:S(2)}) collective-permute-start(bf16[2,32,256]{2,1,0:T(8,128)(2,1)S(1)} %copy-done.49), channel_id=1, source_target_pairs={{0,121},{1,122},{2,123},{3,124},{4,125},{5,126},{6,127},{7,0},{8,1... | collective-permute-start | bytes 98312 | tf_op jit(solution)/shard_map/ppermute | solution.py:319
  54.0 7.5 %collective-permute-start.31 = (bf16[2,32,256]{2,1,0:T(8,128)(2,1)S(1)}, bf16[2,32,256]{2,1,0:T(8,128)(2,1)S(1)}, u32[]{:S(2)}, u32[]{:S(2)}) collective-permute-start(bf16[2,32,256]{2,1,0:T(8,128)(2,1)S(1)} %copy-done.48), channel_id=1, source_target_pairs={{0,120},{1,121},{2,122},{3,123},{4,124},{5,125},{6,126},{7,127},{8... | collective-permute-start | bytes 98312 | tf_op jit(solution)/shard_map/ppermute | solution.py:319
  55.4 9.2 %collective-permute-start = (bf16[2,32,256]{2,1,0:T(8,128)(2,1)}, bf16[2,32,256]{2,1,0:T(8,128)(2,1)S(1)}, u32[]{:S(2)}, u32[]{:S(2)}) collective-permute-start(bf16[2,32,256]{2,1,0:T(8,128)(2,1)} %get-tuple-element.64), channel_id=1, source_target_pairs={{0,8},{1,9},{2,10},{3,11},{4,12},{5,13},{6,14},{7,15},{8,16},{9,17... | collective-permute-start | bytes 98312 | tf_op jit(solution)/shard_map/ppermute | solution.py:319
  55.8 11.6 %collective-permute-start.1 = (bf16[2,32,256]{2,1,0:T(8,128)(2,1)}, bf16[2,32,256]{2,1,0:T(8,128)(2,1)S(1)}, u32[]{:S(2)}, u32[]{:S(2)}) collective-permute-start(bf16[2,32,256]{2,1,0:T(8,128)(2,1)} %get-tuple-element.65), channel_id=1, source_target_pairs={{0,7},{1,8},{2,9},{3,10},{4,11},{5,12},{6,13},{7,14},{8,15},{9,16}... | collective-permute-start | bytes 98312 | tf_op jit(solution)/shard_map/ppermute | solution.py:319
  60.1 9.0 %collective-permute-start.2 = (bf16[2,32,256]{2,1,0:T(8,128)(2,1)}, bf16[2,32,256]{2,1,0:T(8,128)(2,1)S(1)}, u32[]{:S(2)}, u32[]{:S(2)}) collective-permute-start(bf16[2,32,256]{2,1,0:T(8,128)(2,1)} %get-tuple-element.66), channel_id=1, source_target_pairs={{0,6},{1,7},{2,8},{3,9},{4,10},{5,11},{6,12},{7,13},{8,14},{9,15},... | collective-permute-start | bytes 98312 | tf_op jit(solution)/shard_map/ppermute | solution.py:319
  61.4 8.4 %collective-permute-start.3 = (bf16[2,32,256]{2,1,0:T(8,128)(2,1)}, bf16[2,32,256]{2,1,0:T(8,128)(2,1)S(1)}, u32[]{:S(2)}, u32[]{:S(2)}) collective-permute-start(bf16[2,32,256]{2,1,0:T(8,128)(2,1)} %get-tuple-element.67), channel_id=1, source_target_pairs={{0,5},{1,6},{2,7},{3,8},{4,9},{5,10},{6,11},{7,12},{8,13},{9,14},{... | collective-permute-start | bytes 98312 | tf_op jit(solution)/shard_map/ppermute | solution.py:319
  61.5 10.7 %collective-permute-start.4 = (bf16[2,32,256]{2,1,0:T(8,128)(2,1)}, bf16[2,32,256]{2,1,0:T(8,128)(2,1)S(1)}, u32[]{:S(2)}, u32[]{:S(2)}) collective-permute-start(bf16[2,32,256]{2,1,0:T(8,128)(2,1)} %get-tuple-element.68), channel_id=1, source_target_pairs={{0,4},{1,5},{2,6},{3,7},{4,8},{5,9},{6,10},{7,11},{8,12},{9,13},{1... | collective-permute-start | bytes 98312 | tf_op jit(solution)/shard_map/ppermute | solution.py:319
  64.6 9.3 %collective-permute-start.5 = (bf16[2,32,256]{2,1,0:T(8,128)(2,1)}, bf16[2,32,256]{2,1,0:T(8,128)(2,1)S(1)}, u32[]{:S(2)}, u32[]{:S(2)}) collective-permute-start(bf16[2,32,256]{2,1,0:T(8,128)(2,1)} %get-tuple-element.69), channel_id=1, source_target_pairs={{0,3},{1,4},{2,5},{3,6},{4,7},{5,8},{6,9},{7,10},{8,11},{9,12},{10... | collective-permute-start | bytes 98312 | tf_op jit(solution)/shard_map/ppermute | solution.py:319
  67.3 10.7 %collective-permute-start.6 = (bf16[2,32,256]{2,1,0:T(8,128)(2,1)}, bf16[2,32,256]{2,1,0:T(8,128)(2,1)S(1)}, u32[]{:S(2)}, u32[]{:S(2)}) collective-permute-start(bf16[2,32,256]{2,1,0:T(8,128)(2,1)} %get-tuple-element.70), channel_id=1, source_target_pairs={{0,2},{1,3},{2,4},{3,5},{4,6},{5,7},{6,8},{7,9},{8,10},{9,11},{10,... | collective-permute-start | bytes 98312 | tf_op jit(solution)/shard_map/ppermute | solution.py:319
  69.2 9.6 %collective-permute-start.7 = (bf16[2,32,256]{2,1,0:T(8,128)(2,1)}, bf16[2,32,256]{2,1,0:T(8,128)(2,1)S(1)}, u32[]{:S(2)}, u32[]{:S(2)}) collective-permute-start(bf16[2,32,256]{2,1,0:T(8,128)(2,1)} %get-tuple-element.71), channel_id=1, source_target_pairs={{0,1},{1,2},{2,3},{3,4},{4,5},{5,6},{6,7},{7,8},{8,9},{9,10},{10,1... | collective-permute-start | bytes 98312 | tf_op jit(solution)/shard_map/ppermute | solution.py:319
  69.8 9.1 %collective-permute-start.8 = (bf16[2,32,256]{2,1,0:T(8,128)(2,1)}, bf16[2,32,256]{2,1,0:T(8,128)(2,1)S(1)}, u32[]{:S(2)}, u32[]{:S(2)}) collective-permute-start(bf16[2,32,256]{2,1,0:T(8,128)(2,1)} %get-tuple-element.72), channel_id=1, source_target_pairs={{0,127},{1,0},{2,1},{3,2},{4,3},{5,4},{6,5},{7,6},{8,7},{9,8},{10,... | collective-permute-start | bytes 98312 | tf_op jit(solution)/shard_map/ppermute | solution.py:319
  72.1 8.7 %collective-permute-start.9 = (bf16[2,32,256]{2,1,0:T(8,128)(2,1)}, bf16[2,32,256]{2,1,0:T(8,128)(2,1)S(1)}, u32[]{:S(2)}, u32[]{:S(2)}) collective-permute-start(bf16[2,32,256]{2,1,0:T(8,128)(2,1)} %get-tuple-element.73), channel_id=1, source_target_pairs={{0,126},{1,127},{2,0},{3,1},{4,2},{5,3},{6,4},{7,5},{8,6},{9,7},{1... | collective-permute-start | bytes 98312 | tf_op jit(solution)/shard_map/ppermute | solution.py:319
  74.0 6.9 %collective-permute-start.10 = (bf16[2,32,256]{2,1,0:T(8,128)(2,1)}, bf16[2,32,256]{2,1,0:T(8,128)(2,1)S(1)}, u32[]{:S(2)}, u32[]{:S(2)}) collective-permute-start(bf16[2,32,256]{2,1,0:T(8,128)(2,1)} %get-tuple-element.74), channel_id=1, source_target_pairs={{0,125},{1,126},{2,127},{3,0},{4,1},{5,2},{6,3},{7,4},{8,5},{9,6},... | collective-permute-start | bytes 98312 | tf_op jit(solution)/shard_map/ppermute | solution.py:319
  78.0 4.8 %collective-permute-start.11 = (bf16[2,32,256]{2,1,0:T(8,128)(2,1)}, bf16[2,32,256]{2,1,0:T(8,128)(2,1)S(1)}, u32[]{:S(2)}, u32[]{:S(2)}) collective-permute-start(bf16[2,32,256]{2,1,0:T(8,128)(2,1)} %get-tuple-element.75), channel_id=1, source_target_pairs={{0,124},{1,125},{2,126},{3,127},{4,0},{5,1},{6,2},{7,3},{8,4},{9,5... | collective-permute-start | bytes 98312 | tf_op jit(solution)/shard_map/ppermute | solution.py:319
  78.7 4.8 %collective-permute-start.12 = (bf16[2,32,256]{2,1,0:T(8,128)(2,1)}, bf16[2,32,256]{2,1,0:T(8,128)(2,1)S(1)}, u32[]{:S(2)}, u32[]{:S(2)}) collective-permute-start(bf16[2,32,256]{2,1,0:T(8,128)(2,1)} %get-tuple-element.76), channel_id=1, source_target_pairs={{0,123},{1,124},{2,125},{3,126},{4,127},{5,0},{6,1},{7,2},{8,3},{9... | collective-permute-start | bytes 98312 | tf_op jit(solution)/shard_map/ppermute | solution.py:319
  79.0 6.2 %collective-permute-start.13 = (bf16[2,32,256]{2,1,0:T(8,128)(2,1)}, bf16[2,32,256]{2,1,0:T(8,128)(2,1)S(1)}, u32[]{:S(2)}, u32[]{:S(2)}) collective-permute-start(bf16[2,32,256]{2,1,0:T(8,128)(2,1)} %get-tuple-element.77), channel_id=1, source_target_pairs={{0,122},{1,123},{2,124},{3,125},{4,126},{5,127},{6,0},{7,1},{8,2},... | collective-permute-start | bytes 98312 | tf_op jit(solution)/shard_map/ppermute | solution.py:319
  80.8 5.8 %collective-permute-start.14 = (bf16[2,32,256]{2,1,0:T(8,128)(2,1)}, bf16[2,32,256]{2,1,0:T(8,128)(2,1)S(1)}, u32[]{:S(2)}, u32[]{:S(2)}) collective-permute-start(bf16[2,32,256]{2,1,0:T(8,128)(2,1)} %get-tuple-element.78), channel_id=1, source_target_pairs={{0,121},{1,122},{2,123},{3,124},{4,125},{5,126},{6,127},{7,0},{8,1... | collective-permute-start | bytes 98312 | tf_op jit(solution)/shard_map/ppermute | solution.py:319
  80.8 8.5 %collective-permute-start.15 = (bf16[2,32,256]{2,1,0:T(8,128)(2,1)}, bf16[2,32,256]{2,1,0:T(8,128)(2,1)S(1)}, u32[]{:S(2)}, u32[]{:S(2)}) collective-permute-start(bf16[2,32,256]{2,1,0:T(8,128)(2,1)} %get-tuple-element.79), channel_id=1, source_target_pairs={{0,120},{1,121},{2,122},{3,123},{4,124},{5,125},{6,126},{7,127},{8... | collective-permute-start | bytes 98312 | tf_op jit(solution)/shard_map/ppermute | solution.py:319
  137.3 16.7 %collective-permute-start.32 = (bf16[2,32,256]{2,1,0:T(8,128)(2,1)}, bf16[2,32,256]{2,1,0:T(8,128)(2,1)S(1)}, u32[]{:S(2)}, u32[]{:S(2)}) collective-permute-start(bf16[2,32,256]{2,1,0:T(8,128)(2,1)} %get-tuple-element.98), channel_id=1, source_target_pairs={{0,8},{1,9},{2,10},{3,11},{4,12},{5,13},{6,14},{7,15},{8,16},{9,17... | collective-permute-start | bytes 98312 | tf_op jit(solution)/shard_map/ppermute | solution.py:319
  148.5 7.6 %collective-permute-start.33 = (bf16[2,32,256]{2,1,0:T(8,128)(2,1)}, bf16[2,32,256]{2,1,0:T(8,128)(2,1)S(1)}, u32[]{:S(2)}, u32[]{:S(2)}) collective-permute-start(bf16[2,32,256]{2,1,0:T(8,128)(2,1)} %get-tuple-element.99), channel_id=1, source_target_pairs={{0,7},{1,8},{2,9},{3,10},{4,11},{5,12},{6,13},{7,14},{8,15},{9,16}... | collective-permute-start | bytes 98312 | tf_op jit(solution)/shard_map/ppermute | solution.py:319
  149.4 8.7 %collective-permute-start.34 = (bf16[2,32,256]{2,1,0:T(8,128)(2,1)}, bf16[2,32,256]{2,1,0:T(8,128)(2,1)S(1)}, u32[]{:S(2)}, u32[]{:S(2)}) collective-permute-start(bf16[2,32,256]{2,1,0:T(8,128)(2,1)} %get-tuple-element.100), channel_id=1, source_target_pairs={{0,6},{1,7},{2,8},{3,9},{4,10},{5,11},{6,12},{7,13},{8,14},{9,15},... | collective-permute-start | bytes 98312 | tf_op jit(solution)/shard_map/ppermute | solution.py:319
  153.8 8.4 %collective-permute-start.35 = (bf16[2,32,256]{2,1,0:T(8,128)(2,1)}, bf16[2,32,256]{2,1,0:T(8,128)(2,1)S(1)}, u32[]{:S(2)}, u32[]{:S(2)}) collective-permute-start(bf16[2,32,256]{2,1,0:T(8,128)(2,1)} %get-tuple-element.101), channel_id=1, source_target_pairs={{0,5},{1,6},{2,7},{3,8},{4,9},{5,10},{6,11},{7,12},{8,13},{9,14},{... | collective-permute-start | bytes 98312 | tf_op jit(solution)/shard_map/ppermute | solution.py:319
  153.8 8.4 %collective-permute-start.36 = (bf16[2,32,256]{2,1,0:T(8,128)(2,1)}, bf16[2,32,256]{2,1,0:T(8,128)(2,1)S(1)}, u32[]{:S(2)}, u32[]{:S(2)}) collective-permute-start(bf16[2,32,256]{2,1,0:T(8,128)(2,1)} %get-tuple-element.102), channel_id=1, source_target_pairs={{0,4},{1,5},{2,6},{3,7},{4,8},{5,9},{6,10},{7,11},{8,12},{9,13},{1... | collective-permute-start | bytes 98312 | tf_op jit(solution)/shard_map/ppermute | solution.py:319
  154.0 8.4 %collective-permute-start.37 = (bf16[2,32,256]{2,1,0:T(8,128)(2,1)}, bf16[2,32,256]{2,1,0:T(8,128)(2,1)S(1)}, u32[]{:S(2)}, u32[]{:S(2)}) collective-permute-start(bf16[2,32,256]{2,1,0:T(8,128)(2,1)} %get-tuple-element.103), channel_id=1, source_target_pairs={{0,3},{1,4},{2,5},{3,6},{4,7},{5,8},{6,9},{7,10},{8,11},{9,12},{10... | collective-permute-start | bytes 98312 | tf_op jit(solution)/shard_map/ppermute | solution.py:319
  156.1 9.7 %collective-permute-start.38 = (bf16[2,32,256]{2,1,0:T(8,128)(2,1)}, bf16[2,32,256]{2,1,0:T(8,128)(2,1)S(1)}, u32[]{:S(2)}, u32[]{:S(2)}) collective-permute-start(bf16[2,32,256]{2,1,0:T(8,128)(2,1)} %get-tuple-element.104), channel_id=1, source_target_pairs={{0,2},{1,3},{2,4},{3,5},{4,6},{5,7},{6,8},{7,9},{8,10},{9,11},{10,... | collective-permute-start | bytes 98312 | tf_op jit(solution)/shard_map/ppermute | solution.py:319
  158.1 8.4 %collective-permute-start.39 = (bf16[2,32,256]{2,1,0:T(8,128)(2,1)}, bf16[2,32,256]{2,1,0:T(8,128)(2,1)S(1)}, u32[]{:S(2)}, u32[]{:S(2)}) collective-permute-start(bf16[2,32,256]{2,1,0:T(8,128)(2,1)} %get-tuple-element.105), channel_id=1, source_target_pairs={{0,1},{1,2},{2,3},{3,4},{4,5},{5,6},{6,7},{7,8},{8,9},{9,10},{10,1... | collective-permute-start | bytes 98312 | tf_op jit(solution)/shard_map/ppermute | solution.py:319
  162.3 7.9 %collective-permute-start.40 = (bf16[2,32,256]{2,1,0:T(8,128)(2,1)}, bf16[2,32,256]{2,1,0:T(8,128)(2,1)S(1)}, u32[]{:S(2)}, u32[]{:S(2)}) collective-permute-start(bf16[2,32,256]{2,1,0:T(8,128)(2,1)} %get-tuple-element.106), channel_id=1, source_target_pairs={{0,127},{1,0},{2,1},{3,2},{4,3},{5,4},{6,5},{7,6},{8,7},{9,8},{10,... | collective-permute-start | bytes 98312 | tf_op jit(solution)/shard_map/ppermute | solution.py:319
  162.3 7.9 %collective-permute-start.41 = (bf16[2,32,256]{2,1,0:T(8,128)(2,1)}, bf16[2,32,256]{2,1,0:T(8,128)(2,1)S(1)}, u32[]{:S(2)}, u32[]{:S(2)}) collective-permute-start(bf16[2,32,256]{2,1,0:T(8,128)(2,1)} %get-tuple-element.107), channel_id=1, source_target_pairs={{0,126},{1,127},{2,0},{3,1},{4,2},{5,3},{6,4},{7,5},{8,6},{9,7},{1... | collective-permute-start | bytes 98312 | tf_op jit(solution)/shard_map/ppermute | solution.py:319
  162.4 10.1 %collective-permute-start.42 = (bf16[2,32,256]{2,1,0:T(8,128)(2,1)}, bf16[2,32,256]{2,1,0:T(8,128)(2,1)S(1)}, u32[]{:S(2)}, u32[]{:S(2)}) collective-permute-start(bf16[2,32,256]{2,1,0:T(8,128)(2,1)} %get-tuple-element.108), channel_id=1, source_target_pairs={{0,125},{1,126},{2,127},{3,0},{4,1},{5,2},{6,3},{7,4},{8,5},{9,6},... | collective-permute-start | bytes 98312 | tf_op jit(solution)/shard_map/ppermute | solution.py:319
  165.9 9.1 %collective-permute-start.43 = (bf16[2,32,256]{2,1,0:T(8,128)(2,1)}, bf16[2,32,256]{2,1,0:T(8,128)(2,1)S(1)}, u32[]{:S(2)}, u32[]{:S(2)}) collective-permute-start(bf16[2,32,256]{2,1,0:T(8,128)(2,1)} %get-tuple-element.109), channel_id=1, source_target_pairs={{0,124},{1,125},{2,126},{3,127},{4,0},{5,1},{6,2},{7,3},{8,4},{9,5... | collective-permute-start | bytes 98312 | tf_op jit(solution)/shard_map/ppermute | solution.py:319
  166.6 8.4 %collective-permute-start.44 = (bf16[2,32,256]{2,1,0:T(8,128)(2,1)}, bf16[2,32,256]{2,1,0:T(8,128)(2,1)S(1)}, u32[]{:S(2)}, u32[]{:S(2)}) collective-permute-start(bf16[2,32,256]{2,1,0:T(8,128)(2,1)} %get-tuple-element.110), channel_id=1, source_target_pairs={{0,123},{1,124},{2,125},{3,126},{4,127},{5,0},{6,1},{7,2},{8,3},{9... | collective-permute-start | bytes 98312 | tf_op jit(solution)/shard_map/ppermute | solution.py:319
  170.2 6.3 %collective-permute-start.45 = (bf16[2,32,256]{2,1,0:T(8,128)(2,1)}, bf16[2,32,256]{2,1,0:T(8,128)(2,1)S(1)}, u32[]{:S(2)}, u32[]{:S(2)}) collective-permute-start(bf16[2,32,256]{2,1,0:T(8,128)(2,1)} %get-tuple-element.111), channel_id=1, source_target_pairs={{0,122},{1,123},{2,124},{3,125},{4,126},{5,127},{6,0},{7,1},{8,2},... | collective-permute-start | bytes 98312 | tf_op jit(solution)/shard_map/ppermute | solution.py:319
  170.2 6.3 %collective-permute-start.46 = (bf16[2,32,256]{2,1,0:T(8,128)(2,1)}, bf16[2,32,256]{2,1,0:T(8,128)(2,1)S(1)}, u32[]{:S(2)}, u32[]{:S(2)}) collective-permute-start(bf16[2,32,256]{2,1,0:T(8,128)(2,1)} %get-tuple-element.112), channel_id=1, source_target_pairs={{0,121},{1,122},{2,123},{3,124},{4,125},{5,126},{6,127},{7,0},{8,1... | collective-permute-start | bytes 98312 | tf_op jit(solution)/shard_map/ppermute | solution.py:319
  172.5 4.7 %collective-permute-start.47 = (bf16[2,32,256]{2,1,0:T(8,128)(2,1)}, bf16[2,32,256]{2,1,0:T(8,128)(2,1)S(1)}, u32[]{:S(2)}, u32[]{:S(2)}) collective-permute-start(bf16[2,32,256]{2,1,0:T(8,128)(2,1)} %get-tuple-element.113), channel_id=1, source_target_pairs={{0,120},{1,121},{2,122},{3,123},{4,124},{5,125},{6,126},{7,127},{8... | collective-permute-start | bytes 98312 | tf_op jit(solution)/shard_map/ppermute | solution.py:319
  (52 other events, 1280.1 us)
